TPU v7x, 32 devices: a whole 2x2x4 slice. The times are simulated.
32 devices in a mesh: tm: 32 (over z, y, x, core).
Axes of the slice: x: 2, y: 2, z: 4, core: 2. Of those that a mesh axis runs over, the one named last changes fastest.
Arguments:
- queries: bfloat16 [128, 32, 640], P('tm'), may hold values from -8 to 8
- keys: bfloat16 [128, 32, 640], P('tm'), may hold values from -8 to 8
- values: bfloat16 [128, 32, 640], P('tm'), may hold values from -8 to 8
- out_grad: bfloat16 [128, 32, 640], P('tm'), may hold values from -8 to 8
- clip_lengths: int32 [16], replicated, may hold values from 1 to 24, 128 in all
Outputs:
- attended: bfloat16 [128, 32, 640], P('tm')
- grad_queries: bfloat16 [128, 32, 640], P('tm')
- grad_keys: bfloat16 [128, 32, 640], P('tm')
- grad_values: bfloat16 [128, 32, 640], P('tm')
Inputs may be any that keep to these rules, and one draw needn't show every extreme that they name: `clip_lengths`: lengths sum to 128; the longest clip has exactly 24 frames.
All inputs are finite; a program needn't handle non-finite values.
Results may differ from a plain program's by a relative error of at most 0.0088.
Values may be sent and summed in bfloat16 or wider, within the bound.
A program may use at most 64 MiB of HBM per device.

v0:
```python
import jax
import jax.numpy as jnp
from jax import lax
from jax.sharding import PartitionSpec as P

HEADS = 10
MAXCLIP = 24


def as_sent(shard):
    return jax.tree.map(lambda a: a.astype(jnp.bfloat16) if a.dtype == jnp.float32 else a, shard)


def from_behind(value, axis, steps):
    count = lax.axis_size(axis)
    initial, last = (max(0, -steps), min(count, count - steps))
    return lax.ppermute(value, axis, [(source, source + steps) for source in range(initial, last)])


def attend_frame(query, key_cat, value_cat, grad_out):
    tokens = query.shape[0]
    model_width = query.shape[1]
    head_size = model_width // HEADS
    score_scale = head_size ** (-0.5)
    query_heads = query.reshape(tokens, HEADS, head_size)
    key_heads = key_cat.reshape(2 * tokens, HEADS, head_size)
    value_heads = value_cat.reshape(2 * tokens, HEADS, head_size)
    grad_heads = grad_out.reshape(tokens, HEADS, head_size)
    scores = (
        jnp.einsum("qhd,khd->hqk", query_heads, key_heads, preferred_element_type=jnp.float32)
        * score_scale
    )
    row_max = jnp.max(scores, axis=-1, keepdims=True)
    expos = jnp.exp(scores - row_max)
    attn_prob = expos / jnp.sum(expos, axis=-1, keepdims=True)
    prob_low = attn_prob.astype(jnp.bfloat16)
    attended = jnp.einsum("hqk,khd->qhd", prob_low, value_heads, preferred_element_type=jnp.float32)
    attended = attended.reshape(tokens, model_width).astype(jnp.bfloat16)
    grad_prob = jnp.einsum(
        "qhd,khd->hqk", grad_heads, value_heads, preferred_element_type=jnp.float32
    )
    grad_value = jnp.einsum(
        "hqk,qhd->khd", prob_low, grad_heads, preferred_element_type=jnp.float32
    )
    grad_value = grad_value.reshape(2 * tokens, model_width)
    grad_score = (
        attn_prob
        * (grad_prob - jnp.sum(attn_prob * grad_prob, axis=-1, keepdims=True))
        * score_scale
    )
    score_low = grad_score.astype(jnp.bfloat16)
    grad_query = jnp.einsum(
        "hqk,khd->qhd", score_low, key_heads, preferred_element_type=jnp.float32
    )
    grad_query = grad_query.reshape(tokens, model_width).astype(jnp.bfloat16)
    grad_key = jnp.einsum(
        "hqk,qhd->khd", score_low, query_heads, preferred_element_type=jnp.float32
    )
    grad_key = grad_key.reshape(2 * tokens, model_width)
    return (attended, grad_query, grad_key, grad_value)


def take_latest(earlier, later):
    chosen = later[0] > 0
    return (
        jnp.maximum(earlier[0], later[0]),
        jnp.where(chosen, later[1], earlier[1]),
        jnp.where(chosen, later[2], earlier[2]),
    )


def add_segment(earlier, later):
    closed = later[0] > 0
    return (
        jnp.maximum(earlier[0], later[0]),
        later[1] + jnp.where(closed, 0.0, earlier[1]),
        later[2] + jnp.where(closed, 0.0, earlier[2]),
    )


def body(queries, keys, values, out_grad, clip_lengths):
    frame_count = queries.shape[0]
    tokens = queries.shape[1]
    first_frame = lax.axis_index("tm") * frame_count
    frame_ids = first_frame + jnp.arange(frame_count, dtype=jnp.int32)
    clip_ends = jnp.cumsum(clip_lengths)
    clip_starts = clip_ends - clip_lengths
    owner = jnp.max(
        jnp.where(clip_starts[None, :] <= frame_ids[:, None], clip_starts[None, :], 0), axis=1
    )
    opening = owner == frame_ids
    local_owner = owner - first_frame
    has_start = local_owner[frame_count - 1] >= 0
    marker = jnp.where(has_start, 1, 0).astype(jnp.int32).reshape(1)
    last_open = jnp.clip(local_owner[frame_count - 1], 0, frame_count - 1)
    element = (marker, keys[last_open], values[last_open])
    reach_devices = (MAXCLIP + 2) // 4
    rounds = (reach_devices - 1).bit_length()
    carried = element
    for section in range(rounds + 1):
        offset = 1 if section == 0 else 2 ** (section - 1)
        moved = from_behind((as_sent(carried[0]), carried[1], carried[2]), "tm", offset)
        carried = moved if section == 0 else take_latest(moved, carried)
    local_key_index = jnp.clip(local_owner, 0, frame_count - 1)
    owned_here = (local_owner >= 0)[:, None, None]
    key_frames = jnp.where(owned_here, jnp.take(keys, local_key_index, axis=0), carried[1][None])
    value_frames = jnp.where(
        owned_here, jnp.take(values, local_key_index, axis=0), carried[2][None]
    )
    before = from_behind((keys[frame_count - 1], values[frame_count - 1]), "tm", 1)
    prev_keys = jnp.concatenate([before[0][None], keys[: frame_count - 1]], axis=0)
    prev_values = jnp.concatenate([before[1][None], values[: frame_count - 1]], axis=0)
    prev_keys = jnp.where(opening[:, None, None], keys, prev_keys)
    prev_values = jnp.where(opening[:, None, None], values, prev_values)
    attended_list, grad_query_list, grad_key_list, grad_value_list = ([], [], [], [])
    for position in range(frame_count):
        key_cat = jnp.concatenate([key_frames[position], prev_keys[position]], axis=0)
        value_cat = jnp.concatenate([value_frames[position], prev_values[position]], axis=0)
        results = attend_frame(queries[position], key_cat, value_cat, out_grad[position])
        attended_list.append(results[0])
        grad_query_list.append(results[1])
        grad_key_list.append(results[2])
        grad_value_list.append(results[3])
    attended = jnp.stack(attended_list, axis=0)
    grad_queries = jnp.stack(grad_query_list, axis=0)
    key_grads = jnp.stack(grad_key_list, axis=0)
    value_grads = jnp.stack(grad_value_list, axis=0)
    keyframe_gk, prev_gk = (key_grads[:, :tokens], key_grads[:, tokens:])
    keyframe_gv, prev_gv = (value_grads[:, :tokens], value_grads[:, tokens:])
    targets = jnp.arange(frame_count, dtype=jnp.int32)
    to_owner = (local_owner[None, :] == targets[:, None])[:, :, None, None]
    prev_target = jnp.where(opening, targets, targets - 1)
    to_prev = (prev_target[None, :] == targets[:, None])[:, :, None, None]
    acc_key = jnp.sum(jnp.where(to_owner, keyframe_gk[None], 0.0), axis=1) + jnp.sum(
        jnp.where(to_prev, prev_gk[None], 0.0), axis=1
    )
    acc_value = jnp.sum(jnp.where(to_owner, keyframe_gv[None], 0.0), axis=1) + jnp.sum(
        jnp.where(to_prev, prev_gv[None], 0.0), axis=1
    )
    returned = (
        from_behind(jnp.where(opening[0], 0.0, prev_gk[0]).astype(jnp.bfloat16), "tm", -1).astype(
            jnp.float32
        ),
        from_behind(jnp.where(opening[0], 0.0, prev_gv[0]).astype(jnp.bfloat16), "tm", -1).astype(
            jnp.float32
        ),
    )
    acc_key = acc_key.at[frame_count - 1].add(returned[0])
    acc_value = acc_value.at[frame_count - 1].add(returned[1])
    remote = (local_owner < 0)[:, None, None]
    grad_element = (
        marker,
        jnp.sum(jnp.where(remote, keyframe_gk, 0.0), axis=0),
        jnp.sum(jnp.where(remote, keyframe_gv, 0.0), axis=0),
    )
    incoming = grad_element
    for section in range(rounds + 1):
        offset = 1 if section == 0 else 2 ** (section - 1)
        moved = from_behind((incoming[0], incoming[1], incoming[2]), "tm", -offset)
        incoming = moved if section == 0 else add_segment(moved, incoming)
    to_last = jnp.logical_and(targets == last_open, has_start)[:, None, None]
    acc_key = acc_key + jnp.where(to_last, incoming[1][None], 0.0)
    acc_value = acc_value + jnp.where(to_last, incoming[2][None], 0.0)
    return (attended, grad_queries, acc_key.astype(jnp.bfloat16), acc_value.astype(jnp.bfloat16))


def solution(mesh):
    in_specs = (
        P("tm", None, None),
        P("tm", None, None),
        P("tm", None, None),
        P("tm", None, None),
        P(),
    )
    out_specs = (P("tm", None, None), P("tm", None, None), P("tm", None, None), P("tm", None, None))
    return jax.shard_map(body, mesh=mesh, in_specs=in_specs, out_specs=out_specs, check_vma=False)
```

profile of v0, /device:TPU:19, one launch (start us, length us, event | category | flops | bytes accessed | tf_op | source)
XLA Modules:
  0.0 153.5 jit_solution(1555710741188852860)
XLA Ops:
  3.7 4.4 %collective-permute-start = (s32[1]{0:T(128)}, s32[1]{0:T(128)}, u32[]{:S(2)}, u32[]{:S(2)}) collective-permute-start(s32[1]{0:T(128)} %bitcast.2), channel_id=1, source_target_pairs={{0,1},{1,2},{2,3},{3,4},{4,5},{5,6},{6,7},{7,8},{8,9},{9,10},{10,1... | collective-permute-start | bytes 20 | tf_op jit(solution)/shard_map/ppermute | solution.py:17
  8.1 2.7 %collective-permute-start.15 = (s32[1]{0:T(128)}, s32[1]{0:T(128)}, u32[]{:S(2)}, u32[]{:S(2)}) collective-permute-start(s32[1]{0:T(128)} %bitcast.2), channel_id=1, source_target_pairs={{1,0},{2,1},{3,2},{4,3},{5,4},{6,5},{7,6},{8,7},{9,8},{10,9},{11,1... | collective-permute-start | bytes 20 | tf_op jit(solution)/shard_map/ppermute | solution.py:17
  12.3 5.0 %collective-permute-start.8 = (bf16[32,640]{1,0:T(8,128)(2,1)S(1)}, bf16[32,640]{1,0:T(8,128)(2,1)S(1)}, u32[]{:S(2)}, u32[]{:S(2)}) collective-permute-start(bf16[32,640]{1,0:T(8,128)(2,1)S(1)} %get-tuple-element.74), channel_id=1, source_target_pairs={{0,1},{1,2},{2,3},{3,4},{4,5},{5,6},{6,7},{7,8},{8,9},{9,10},{10,1... | collective-permute-start | bytes 122888 | tf_op jit(solution)/shard_map/ppermute | solution.py:17
  20.1 2.6 %collective-permute-start.7 = (bf16[32,640]{1,0:T(8,128)(2,1)S(1)}, bf16[32,640]{1,0:T(8,128)(2,1)S(1)}, u32[]{:S(2)}, u32[]{:S(2)}) collective-permute-start(bf16[32,640]{1,0:T(8,128)(2,1)S(1)} %get-tuple-element.75), channel_id=1, source_target_pairs={{0,1},{1,2},{2,3},{3,4},{4,5},{5,6},{6,7},{7,8},{8,9},{9,10},{10,1... | collective-permute-start | bytes 122888 | tf_op jit(solution)/shard_map/ppermute | solution.py:17
  30.1 5.3 %collective-permute-start.1 = (s32[1]{0:T(128)}, s32[1]{0:T(128)}, u32[]{:S(2)}, u32[]{:S(2)}) collective-permute-start(s32[1]{0:T(128)} %collective-permute-done), channel_id=1, source_target_pairs={{0,1},{1,2},{2,3},{3,4},{4,5},{5,6},{6,7},{7,8},{8,9},{9,10},{10,1... | collective-permute-start | bytes 20 | tf_op jit(solution)/shard_map/ppermute | solution.py:17
  39.3 3.1 %collective-permute-done.17 = s32[1]{0:T(128)} collective-permute-done((s32[1]{0:T(128)}, s32[1]{0:T(128)}, u32[]{:S(2)}, u32[]{:S(2)}) %collective-permute-start.17) | collective-permute-done | bytes 36 | tf_op jit(solution)/shard_map/ppermute | solution.py:17
  42.4 2.7 %collective-permute-start.2 = (s32[1]{0:T(128)}, s32[1]{0:T(128)}, u32[]{:S(2)}, u32[]{:S(2)}) collective-permute-start(s32[1]{0:T(128)} %max.21), channel_id=1, source_target_pairs={{0,2},{1,3},{2,4},{3,5},{4,6},{5,7},{6,8},{7,9},{8,10},{9,11},{10,... | collective-permute-start | bytes 20 | tf_op jit(solution)/shard_map/ppermute | solution.py:17
  46.7 3.8 %collective-permute-start.19 = (s32[1]{0:T(128)}, s32[1]{0:T(128)}, u32[]{:S(2)}, u32[]{:S(2)}) collective-permute-start(s32[1]{0:T(128)} %max.24), channel_id=1, source_target_pairs={{2,0},{3,1},{4,2},{5,3},{6,4},{7,5},{8,6},{9,7},{10,8},{11,9},{12,... | collective-permute-start | bytes 20 | tf_op jit(solution)/shard_map/ppermute | solution.py:17
  52.8 4.3 %collective-permute-start.9 = (bf16[32,640]{1,0:T(8,128)(2,1)S(1)}, bf16[32,640]{1,0:T(8,128)(2,1)S(1)}, u32[]{:S(2)}, u32[]{:S(2)}) collective-permute-start(bf16[32,640]{1,0:T(8,128)(2,1)S(1)} %collective-permute-done.8), channel_id=1, source_target_pairs={{0,1},{1,2},{2,3},{3,4},{4,5},{5,6},{6,7},{7,8},{8,9},{9,10},{10,1... | collective-permute-start | bytes 122888 | tf_op jit(solution)/shard_map/ppermute | solution.py:17
  60.4 4.5 %collective-permute-start.10 = (bf16[32,640]{1,0:T(8,128)(2,1)S(1)}, bf16[32,640]{1,0:T(8,128)(2,1)S(1)}, u32[]{:S(2)}, u32[]{:S(2)}) collective-permute-start(bf16[32,640]{1,0:T(8,128)(2,1)S(1)} %broadcast_select_fusion), channel_id=1, source_target_pairs={{0,2},{1,3},{2,4},{3,5},{4,6},{5,7},{6,8},{7,9},{8,10},{9,11},{10,... | collective-permute-start | bytes 122888 | tf_op jit(solution)/shard_map/ppermute | solution.py:17
  64.9 2.6 %collective-permute-start.5 = (bf16[32,640]{1,0:T(8,128)(2,1)S(1)}, bf16[32,640]{1,0:T(8,128)(2,1)S(1)}, u32[]{:S(2)}, u32[]{:S(2)}) collective-permute-start(bf16[32,640]{1,0:T(8,128)(2,1)S(1)} %broadcast_select_fusion.1), channel_id=1, source_target_pairs={{0,2},{1,3},{2,4},{3,5},{4,6},{5,7},{6,8},{7,9},{8,10},{9,11},{10,... | collective-permute-start | bytes 122888 | tf_op jit(solution)/shard_map/ppermute | solution.py:17
  69.7 2.1 %collective-permute-start.6 = (bf16[32,640]{1,0:T(8,128)(2,1)S(1)}, bf16[32,640]{1,0:T(8,128)(2,1)S(1)}, u32[]{:S(2)}, u32[]{:S(2)}) collective-permute-start(bf16[32,640]{1,0:T(8,128)(2,1)S(1)} %broadcast_select_fusion.3), channel_id=1, source_target_pairs={{0,4},{1,5},{2,6},{3,7},{4,8},{5,9},{6,10},{7,11},{8,12},{9,13},{1... | collective-permute-start | bytes 122888 | tf_op jit(solution)/shard_map/ppermute | solution.py:17
  73.2 2.1 %collective-permute-done.6 = bf16[32,640]{1,0:T(8,128)(2,1)S(1)} collective-permute-done((bf16[32,640]{1,0:T(8,128)(2,1)S(1)}, bf16[32,640]{1,0:T(8,128)(2,1)S(1)}, u32[]{:S(2)}, u32[]{:S(2)}) %collective-permute-start.6) | collective-permute-done | bytes 40992 | tf_op jit(solution)/shard_map/ppermute | solution.py:17
  94.2 2.4 %convolution_bitcast_fusion.4 = f32[64,10,64]{2,0,1:T(8,128)} fusion(f32[10,32,64]{2,1,0:T(8,128)S(1)} %copy-done.8, bf16[32,10,64]{2,1,0:T(8,128)(2,1)S(1)} %reshape_squeeze.27, f32[10,32,64]{2,1,0:T(8,128)S(1)} %copy-done.12, f32[10,32]{1,0:T(8,128)S(1)} %get-tuple-element.84), kind=kOutput, calls=%fused_computation.18 | convolution fusion | flops 2765183 | bytes 369920 | tf_op jit(solution)/shard_map/hqk,qhd->khd/dot_general | solution.py:56
  97.9 2.4 %convolution_bitcast_fusion.5 = f32[64,10,64]{2,0,1:T(8,128)} fusion(f32[10,32,64]{2,1,0:T(8,128)S(1)} %copy-done.9, bf16[32,10,64]{2,1,0:T(8,128)(2,1)S(1)} %reshape_squeeze.26, f32[10,32,64]{2,1,0:T(8,128)S(1)} %copy-done.13, f32[10,32]{1,0:T(8,128)S(1)} %get-tuple-element.86), kind=kOutput, calls=%fused_computation.19 | convolution fusion | flops 2765183 | bytes 369920 | tf_op jit(solution)/shard_map/hqk,qhd->khd/dot_general | solution.py:56
  104.8 2.4 %convolution_bitcast_fusion.7 = f32[64,10,64]{2,0,1:T(8,128)} fusion(f32[10,32,64]{2,1,0:T(8,128)S(1)} %copy-done.10, bf16[32,10,64]{2,1,0:T(8,128)(2,1)S(1)} %reshape_squeeze.24, f32[10,32,64]{2,1,0:T(8,128)S(1)} %copy-done.15, f32[10,32]{1,0:T(8,128)S(1)} %get-tuple-element.90), kind=kOutput, calls=%fused_computation.21 | convolution fusion | flops 2765183 | bytes 369920 | tf_op jit(solution)/shard_map/hqk,qhd->khd/dot_general | solution.py:56
  114.2 5.6 %collective-permute-start.21 = (bf16[32,640]{1,0:T(8,128)(2,1)S(1)}, bf16[32,640]{1,0:T(8,128)(2,1)S(1)}, u32[]{:S(2)}, u32[]{:S(2)}) collective-permute-start(bf16[32,640]{1,0:T(8,128)(2,1)S(1)} %fusion.89), channel_id=1, source_target_pairs={{1,0},{2,1},{3,2},{4,3},{5,4},{6,5},{7,6},{8,7},{9,8},{10,9},{11,1... | collective-permute-start | bytes 122888 | tf_op jit(solution)/shard_map/ppermute | solution.py:17
  122.1 3.4 %collective-permute-start.13 = (bf16[32,640]{1,0:T(8,128)(2,1)S(1)}, bf16[32,640]{1,0:T(8,128)(2,1)S(1)}, u32[]{:S(2)}, u32[]{:S(2)}) collective-permute-start(bf16[32,640]{1,0:T(8,128)(2,1)S(1)} %fusion.88), channel_id=1, source_target_pairs={{1,0},{2,1},{3,2},{4,3},{5,4},{6,5},{7,6},{8,7},{9,8},{10,9},{11,1... | collective-permute-start | bytes 122888 | tf_op jit(solution)/shard_map/ppermute | solution.py:17
  129.9 2.5 %collective-permute-start.23 = (f32[32,640]{1,0:T(8,128)S(1)}, f32[32,640]{1,0:T(8,128)S(1)}, u32[]{:S(2)}, u32[]{:S(2)}) collective-permute-start(f32[32,640]{1,0:T(8,128)S(1)} %collective-permute-done.22), channel_id=1, source_target_pairs={{1,0},{2,1},{3,2},{4,3},{5,4},{6,5},{7,6},{8,7},{9,8},{10,9},{11,1... | collective-permute-start | bytes 245768 | tf_op jit(solution)/shard_map/ppermute | solution.py:17
  134.3 2.2 %collective-permute-done.23 = f32[32,640]{1,0:T(8,128)S(1)} collective-permute-done((f32[32,640]{1,0:T(8,128)S(1)}, f32[32,640]{1,0:T(8,128)S(1)}, u32[]{:S(2)}, u32[]{:S(2)}) %collective-permute-start.23) | collective-permute-done | bytes 81952 | tf_op jit(solution)/shard_map/ppermute | solution.py:17
  139.1 4.0 %collective-permute-start.18 = (f32[32,640]{1,0:T(8,128)S(1)}, f32[32,640]{1,0:T(8,128)S(1)}, u32[]{:S(2)}, u32[]{:S(2)}) collective-permute-start(f32[32,640]{1,0:T(8,128)S(1)} %select_add_fusion.5), channel_id=1, source_target_pairs={{2,0},{3,1},{4,2},{5,3},{6,4},{7,5},{8,6},{9,7},{10,8},{11,9},{12,... | collective-permute-start | bytes 245768 | tf_op jit(solution)/shard_map/ppermute | solution.py:17
  143.6 3.7 %collective-permute-start.25 = (f32[32,640]{1,0:T(8,128)S(1)}, f32[32,640]{1,0:T(8,128)S(1)}, u32[]{:S(2)}, u32[]{:S(2)}) collective-permute-start(f32[32,640]{1,0:T(8,128)S(1)} %select_add_fusion.1), channel_id=1, source_target_pairs={{4,0},{5,1},{6,2},{7,3},{8,4},{9,5},{10,6},{11,7},{12,8},{13,9},{1... | collective-permute-start | bytes 245768 | tf_op jit(solution)/shard_map/ppermute | solution.py:17
  147.4 2.8 %collective-permute-start.20 = (f32[32,640]{1,0:T(8,128)S(1)}, f32[32,640]{1,0:T(8,128)S(1)}, u32[]{:S(2)}, u32[]{:S(2)}) collective-permute-start(f32[32,640]{1,0:T(8,128)S(1)} %select_add_fusion.4), channel_id=1, source_target_pairs={{4,0},{5,1},{6,2},{7,3},{8,4},{9,5},{10,6},{11,7},{12,8},{13,9},{1... | collective-permute-start | bytes 245768 | tf_op jit(solution)/shard_map/ppermute | solution.py:17
  150.2 2.4 %collective-permute-done.20 = f32[32,640]{1,0:T(8,128)S(1)} collective-permute-done((f32[32,640]{1,0:T(8,128)S(1)}, f32[32,640]{1,0:T(8,128)S(1)}, u32[]{:S(2)}, u32[]{:S(2)}) %collective-permute-start.20) | collective-permute-done | bytes 81952 | tf_op jit(solution)/shard_map/ppermute | solution.py:17
  (228 shorter events, 66.5 us)
Async XLA Ops:
  3.7 23.9 %collective-permute-start = (s32[1]{0:T(128)}, s32[1]{0:T(128)}, u32[]{:S(2)}, u32[]{:S(2)}) collective-permute-start(s32[1]{0:T(128)} %bitcast.2), channel_id=1, source_target_pairs={{0,1},{1,2},{2,3},{3,4},{4,5},{5,6},{6,7},{7,8},{8,9},{9,10},{10,1... | collective-permute-start | bytes 20 | tf_op jit(solution)/shard_map/ppermute | solution.py:17
  8.1 22.0 %collective-permute-start.15 = (s32[1]{0:T(128)}, s32[1]{0:T(128)}, u32[]{:S(2)}, u32[]{:S(2)}) collective-permute-start(s32[1]{0:T(128)} %bitcast.2), channel_id=1, source_target_pairs={{1,0},{2,1},{3,2},{4,3},{5,4},{6,5},{7,6},{8,7},{9,8},{10,9},{11,1... | collective-permute-start | bytes 20 | tf_op jit(solution)/shard_map/ppermute | solution.py:17
  12.3 40.5 %collective-permute-start.8 = (bf16[32,640]{1,0:T(8,128)(2,1)S(1)}, bf16[32,640]{1,0:T(8,128)(2,1)S(1)}, u32[]{:S(2)}, u32[]{:S(2)}) collective-permute-start(bf16[32,640]{1,0:T(8,128)(2,1)S(1)} %get-tuple-element.74), channel_id=1, source_target_pairs={{0,1},{1,2},{2,3},{3,4},{4,5},{5,6},{6,7},{7,8},{8,9},{9,10},{10,1... | collective-permute-start | bytes 122888 | tf_op jit(solution)/shard_map/ppermute | solution.py:17
  17.3 35.3 %collective-permute-start.12 = (bf16[32,640]{1,0:T(8,128)(2,1)S(1)}, bf16[32,640]{1,0:T(8,128)(2,1)S(1)}, u32[]{:S(2)}, u32[]{:S(2)}) collective-permute-start(bf16[32,640]{1,0:T(8,128)(2,1)S(1)} %get-tuple-element.73), channel_id=1, source_target_pairs={{0,1},{1,2},{2,3},{3,4},{4,5},{5,6},{6,7},{7,8},{8,9},{9,10},{10,1... | collective-permute-start | bytes 122888 | tf_op jit(solution)/shard_map/ppermute | solution.py:17
  20.1 32.6 %collective-permute-start.7 = (bf16[32,640]{1,0:T(8,128)(2,1)S(1)}, bf16[32,640]{1,0:T(8,128)(2,1)S(1)}, u32[]{:S(2)}, u32[]{:S(2)}) collective-permute-start(bf16[32,640]{1,0:T(8,128)(2,1)S(1)} %get-tuple-element.75), channel_id=1, source_target_pairs={{0,1},{1,2},{2,3},{3,4},{4,5},{5,6},{6,7},{7,8},{8,9},{9,10},{10,1... | collective-permute-start | bytes 122888 | tf_op jit(solution)/shard_map/ppermute | solution.py:17
  27.7 30.8 %collective-permute-start.3 = (bf16[32,640]{1,0:T(8,128)(2,1)S(1)}, bf16[32,640]{1,0:T(8,128)(2,1)S(1)}, u32[]{:S(2)}, u32[]{:S(2)}) collective-permute-start(bf16[32,640]{1,0:T(8,128)(2,1)S(1)} %get-tuple-element.76), channel_id=1, source_target_pairs={{0,1},{1,2},{2,3},{3,4},{4,5},{5,6},{6,7},{7,8},{8,9},{9,10},{10,1... | collective-permute-start | bytes 122888 | tf_op jit(solution)/shard_map/ppermute | solution.py:17
  30.1 6.1 %collective-permute-start.1 = (s32[1]{0:T(128)}, s32[1]{0:T(128)}, u32[]{:S(2)}, u32[]{:S(2)}) collective-permute-start(s32[1]{0:T(128)} %collective-permute-done), channel_id=1, source_target_pairs={{0,1},{1,2},{2,3},{3,4},{4,5},{5,6},{6,7},{7,8},{8,9},{9,10},{10,1... | collective-permute-start | bytes 20 | tf_op jit(solution)/shard_map/ppermute | solution.py:17
  36.2 6.2 %collective-permute-start.17 = (s32[1]{0:T(128)}, s32[1]{0:T(128)}, u32[]{:S(2)}, u32[]{:S(2)}) collective-permute-start(s32[1]{0:T(128)} %collective-permute-done.15), channel_id=1, source_target_pairs={{1,0},{2,1},{3,2},{4,3},{5,4},{6,5},{7,6},{8,7},{9,8},{10,9},{11,1... | collective-permute-start | bytes 20 | tf_op jit(solution)/shard_map/ppermute | solution.py:17
  46.7 5.3 %collective-permute-start.19 = (s32[1]{0:T(128)}, s32[1]{0:T(128)}, u32[]{:S(2)}, u32[]{:S(2)}) collective-permute-start(s32[1]{0:T(128)} %max.24), channel_id=1, source_target_pairs={{2,0},{3,1},{4,2},{5,3},{6,4},{7,5},{8,6},{9,7},{10,8},{11,9},{12,... | collective-permute-start | bytes 20 | tf_op jit(solution)/shard_map/ppermute | solution.py:17
  52.8 7.5 %collective-permute-start.9 = (bf16[32,640]{1,0:T(8,128)(2,1)S(1)}, bf16[32,640]{1,0:T(8,128)(2,1)S(1)}, u32[]{:S(2)}, u32[]{:S(2)}) collective-permute-start(bf16[32,640]{1,0:T(8,128)(2,1)S(1)} %collective-permute-done.8), channel_id=1, source_target_pairs={{0,1},{1,2},{2,3},{3,4},{4,5},{5,6},{6,7},{7,8},{8,9},{9,10},{10,1... | collective-permute-start | bytes 122888 | tf_op jit(solution)/shard_map/ppermute | solution.py:17
  58.4 6.5 %collective-permute-start.4 = (bf16[32,640]{1,0:T(8,128)(2,1)S(1)}, bf16[32,640]{1,0:T(8,128)(2,1)S(1)}, u32[]{:S(2)}, u32[]{:S(2)}) collective-permute-start(bf16[32,640]{1,0:T(8,128)(2,1)S(1)} %collective-permute-done.3), channel_id=1, source_target_pairs={{0,1},{1,2},{2,3},{3,4},{4,5},{5,6},{6,7},{7,8},{8,9},{9,10},{10,1... | collective-permute-start | bytes 122888 | tf_op jit(solution)/shard_map/ppermute | solution.py:17
  60.4 7.2 %collective-permute-start.10 = (bf16[32,640]{1,0:T(8,128)(2,1)S(1)}, bf16[32,640]{1,0:T(8,128)(2,1)S(1)}, u32[]{:S(2)}, u32[]{:S(2)}) collective-permute-start(bf16[32,640]{1,0:T(8,128)(2,1)S(1)} %broadcast_select_fusion), channel_id=1, source_target_pairs={{0,2},{1,3},{2,4},{3,5},{4,6},{5,7},{6,8},{7,9},{8,10},{9,11},{10,... | collective-permute-start | bytes 122888 | tf_op jit(solution)/shard_map/ppermute | solution.py:17
  67.6 5.6 %collective-permute-start.11 = (bf16[32,640]{1,0:T(8,128)(2,1)S(1)}, bf16[32,640]{1,0:T(8,128)(2,1)S(1)}, u32[]{:S(2)}, u32[]{:S(2)}) collective-permute-start(bf16[32,640]{1,0:T(8,128)(2,1)S(1)} %broadcast_select_fusion.2), channel_id=1, source_target_pairs={{0,4},{1,5},{2,6},{3,7},{4,8},{5,9},{6,10},{7,11},{8,12},{9,13},{1... | collective-permute-start | bytes 122888 | tf_op jit(solution)/shard_map/ppermute | solution.py:17
  69.7 5.6 %collective-permute-start.6 = (bf16[32,640]{1,0:T(8,128)(2,1)S(1)}, bf16[32,640]{1,0:T(8,128)(2,1)S(1)}, u32[]{:S(2)}, u32[]{:S(2)}) collective-permute-start(bf16[32,640]{1,0:T(8,128)(2,1)S(1)} %broadcast_select_fusion.3), channel_id=1, source_target_pairs={{0,4},{1,5},{2,6},{3,7},{4,8},{5,9},{6,10},{7,11},{8,12},{9,13},{1... | collective-permute-start | bytes 122888 | tf_op jit(solution)/shard_map/ppermute | solution.py:17
  114.2 15.6 %collective-permute-start.21 = (bf16[32,640]{1,0:T(8,128)(2,1)S(1)}, bf16[32,640]{1,0:T(8,128)(2,1)S(1)}, u32[]{:S(2)}, u32[]{:S(2)}) collective-permute-start(bf16[32,640]{1,0:T(8,128)(2,1)S(1)} %fusion.89), channel_id=1, source_target_pairs={{1,0},{2,1},{3,2},{4,3},{5,4},{6,5},{7,6},{8,7},{9,8},{10,9},{11,1... | collective-permute-start | bytes 122888 | tf_op jit(solution)/shard_map/ppermute | solution.py:17
  120.2 9.7 %collective-permute-start.22 = (f32[32,640]{1,0:T(8,128)S(1)}, f32[32,640]{1,0:T(8,128)S(1)}, u32[]{:S(2)}, u32[]{:S(2)}) collective-permute-start(f32[32,640]{1,0:T(8,128)S(1)} %get-tuple-element.33), channel_id=1, source_target_pairs={{1,0},{2,1},{3,2},{4,3},{5,4},{6,5},{7,6},{8,7},{9,8},{10,9},{11,1... | collective-permute-start | bytes 245768 | tf_op jit(solution)/shard_map/ppermute | solution.py:17
  122.1 10.2 %collective-permute-start.13 = (bf16[32,640]{1,0:T(8,128)(2,1)S(1)}, bf16[32,640]{1,0:T(8,128)(2,1)S(1)}, u32[]{:S(2)}, u32[]{:S(2)}) collective-permute-start(bf16[32,640]{1,0:T(8,128)(2,1)S(1)} %fusion.88), channel_id=1, source_target_pairs={{1,0},{2,1},{3,2},{4,3},{5,4},{6,5},{7,6},{8,7},{9,8},{10,9},{11,1... | collective-permute-start | bytes 122888 | tf_op jit(solution)/shard_map/ppermute | solution.py:17
  125.5 6.9 %collective-permute-start.14 = (f32[32,640]{1,0:T(8,128)S(1)}, f32[32,640]{1,0:T(8,128)S(1)}, u32[]{:S(2)}, u32[]{:S(2)}) collective-permute-start(f32[32,640]{1,0:T(8,128)S(1)} %get-tuple-element.34), channel_id=1, source_target_pairs={{1,0},{2,1},{3,2},{4,3},{5,4},{6,5},{7,6},{8,7},{9,8},{10,9},{11,1... | collective-permute-start | bytes 245768 | tf_op jit(solution)/shard_map/ppermute | solution.py:17
  129.9 6.7 %collective-permute-start.23 = (f32[32,640]{1,0:T(8,128)S(1)}, f32[32,640]{1,0:T(8,128)S(1)}, u32[]{:S(2)}, u32[]{:S(2)}) collective-permute-start(f32[32,640]{1,0:T(8,128)S(1)} %collective-permute-done.22), channel_id=1, source_target_pairs={{1,0},{2,1},{3,2},{4,3},{5,4},{6,5},{7,6},{8,7},{9,8},{10,9},{11,1... | collective-permute-start | bytes 245768 | tf_op jit(solution)/shard_map/ppermute | solution.py:17
  132.4 6.7 %collective-permute-start.16 = (f32[32,640]{1,0:T(8,128)S(1)}, f32[32,640]{1,0:T(8,128)S(1)}, u32[]{:S(2)}, u32[]{:S(2)}) collective-permute-start(f32[32,640]{1,0:T(8,128)S(1)} %collective-permute-done.14), channel_id=1, source_target_pairs={{1,0},{2,1},{3,2},{4,3},{5,4},{6,5},{7,6},{8,7},{9,8},{10,9},{11,1... | collective-permute-start | bytes 245768 | tf_op jit(solution)/shard_map/ppermute | solution.py:17
  136.6 7.1 %collective-permute-start.24 = (f32[32,640]{1,0:T(8,128)S(1)}, f32[32,640]{1,0:T(8,128)S(1)}, u32[]{:S(2)}, u32[]{:S(2)}) collective-permute-start(f32[32,640]{1,0:T(8,128)S(1)} %select_add_fusion.2), channel_id=1, source_target_pairs={{2,0},{3,1},{4,2},{5,3},{6,4},{7,5},{8,6},{9,7},{10,8},{11,9},{12,... | collective-permute-start | bytes 245768 | tf_op jit(solution)/shard_map/ppermute | solution.py:17
  139.1 8.3 %collective-permute-start.18 = (f32[32,640]{1,0:T(8,128)S(1)}, f32[32,640]{1,0:T(8,128)S(1)}, u32[]{:S(2)}, u32[]{:S(2)}) collective-permute-start(f32[32,640]{1,0:T(8,128)S(1)} %select_add_fusion.5), channel_id=1, source_target_pairs={{2,0},{3,1},{4,2},{5,3},{6,4},{7,5},{8,6},{9,7},{10,8},{11,9},{12,... | collective-permute-start | bytes 245768 | tf_op jit(solution)/shard_map/ppermute | solution.py:17
  143.6 6.5 %collective-permute-start.25 = (f32[32,640]{1,0:T(8,128)S(1)}, f32[32,640]{1,0:T(8,128)S(1)}, u32[]{:S(2)}, u32[]{:S(2)}) collective-permute-start(f32[32,640]{1,0:T(8,128)S(1)} %select_add_fusion.1), channel_id=1, source_target_pairs={{4,0},{5,1},{6,2},{7,3},{8,4},{9,5},{10,6},{11,7},{12,8},{13,9},{1... | collective-permute-start | bytes 245768 | tf_op jit(solution)/shard_map/ppermute | solution.py:17
  147.4 5.2 %collective-permute-start.20 = (f32[32,640]{1,0:T(8,128)S(1)}, f32[32,640]{1,0:T(8,128)S(1)}, u32[]{:S(2)}, u32[]{:S(2)}) collective-permute-start(f32[32,640]{1,0:T(8,128)S(1)} %select_add_fusion.4), channel_id=1, source_target_pairs={{4,0},{5,1},{6,2},{7,3},{8,4},{9,5},{10,6},{11,7},{12,8},{13,9},{1... | collective-permute-start | bytes 245768 | tf_op jit(solution)/shard_map/ppermute | solution.py:17
  (27 other events, 223.7 us)
where the time goes:
time: 157 us; the launch traced here: 153 us
  starting transfers between devices  79.3 us (51%)
  matrix products  26.4 us (17%)
  local copies, waits for them, and re-layouts  16.4 us (10%)
  waiting for transfers between devices  13.7 us (9%)
  other arithmetic  9.53 us (6%)
  between operations  8.11 us (5%)
    ppermute x26, starting transfers between devices, from_behind(): lax.ppermute(value, axis, [(source, source + steps) for source in range(i...  79.3 us
    ppermute x26, waiting for transfers between devices, from_behind(): lax.ppermute(value, axis, [(source, source + steps) for source in range(i...  13.7 us
    dot_general x4, matrix products, attend_frame(): jnp.einsum('hqk,qhd->khd', score_low, query_heads, preferred_element_type...  8.73 us
    dot_general x4, matrix products, attend_frame(): jnp.einsum('hqk,khd->qhd', score_low, key_heads, preferred_element_type=j...  6.34 us
    dot_general x4, matrix products, attend_frame(): jnp.einsum('hqk,khd->qhd', prob_low, value_heads, preferred_element_type=...  4.31 us
    unnamed x54, local copies, waits for them, and re-layouts  3.9 us
    dot_general x4, matrix products, attend_frame(): jnp.einsum('hqk,qhd->khd', prob_low, grad_heads, preferred_element_type=j...  3.54 us
    sub x4, other arithmetic, attend_frame(): expos = jnp.exp(scores - row_max)  3.27 us
  transfers between devices with their start and end apart: 26, of which 11 were waited for; matrix products, arithmetic and copies ran while one was open for 7% of the time, Pallas kernels for 0%

commit v1 on v0

v1 whole, which is shorter than its diff:
```python
import functools

import jax
import jax.numpy as jnp
from jax import lax
from jax.experimental import pallas as pl
from jax.experimental.pallas import tpu as pltpu
from jax.sharding import PartitionSpec as P

HEADS = 10
MAXCLIP = 24
MESH = pl.DeviceIdType.MESH


def lane_groups(width, head):
    step = max(256, head)
    return [(start, min(step, width - start)) for start in range(0, width, step)]


def kernel(
    n, reach, groups, head,
    len_ref, q_ref, k_ref, v_ref, g_ref,
    att_ref, gq_ref, gk_ref, gv_ref,
    acc_k, acc_v, fsend, frecv, bsend, brecv, *bufs,
):
    count = len(groups)
    outs, pools = bufs[:count], bufs[count : 2 * count]
    gouts, gins = bufs[2 * count : 3 * count], bufs[3 * count : 4 * count]
    frames, tokens, _ = q_ref.shape
    me = lax.axis_index("tm")
    scale = head ** (-0.5)

    barrier = pltpu.get_barrier_semaphore()
    for k in range(1, reach + 1):
        @pl.when(me + k < n)
        def _():
            pl.semaphore_signal(barrier, inc=1, device_id=(me + k,), device_id_type=MESH)

        @pl.when(me >= k)
        def _():
            pl.semaphore_signal(barrier, inc=1, device_id=(me - k,), device_id_type=MESH)

    first = me * frames
    wanted = [first + f for f in range(frames)]
    wanted += [first + k * frames for k in range(1, reach + 1)]

    def scan_clips(c, carry):
        start, owners = carry
        owners = tuple(jnp.where(start <= w, start, o) for w, o in zip(wanted, owners))
        return start + len_ref[c], owners

    zero = jnp.int32(0)
    _, owners = lax.fori_loop(0, len_ref.shape[0], scan_clips, (zero, (zero,) * len(wanted)))
    local = [owners[f] - first for f in range(frames)]
    opening = [local[f] == f for f in range(frames)]
    has_start = local[frames - 1] >= 0
    last_open = jnp.clip(local[frames - 1], 0, frames - 1)
    back = jnp.clip(me - lax.div(owners[0], jnp.int32(frames)), 1, reach)
    owner_slot = [jnp.where(local[f] >= 0, local[f], frames + back) for f in range(frames)]
    prev_slot = [
        jnp.where(opening[f], f, f - 1 if f else frames) for f in range(frames)
    ]
    returns = []
    for k in range(1, reach + 1):
        owner = owners[frames + k - 1]
        mine = jnp.logical_and(owner >= first, owner < first + frames)
        returns.append(jnp.logical_and(mine, me + k < n))
    next_prev = jnp.logical_and(owners[frames] != first + frames, me + 1 < n)

    for i, (lo, w) in enumerate(groups):
        cols = slice(lo, lo + w)
        outs[i][0, 0] = k_ref[frames - 1, :, cols]
        outs[i][0, 1] = v_ref[frames - 1, :, cols]
        outs[i][1, 0] = k_ref[last_open, :, cols]
        outs[i][1, 1] = v_ref[last_open, :, cols]

    count_all = jnp.minimum(reach, n - 1 - me) + jnp.minimum(reach, me)
    pl.semaphore_wait(barrier, count_all)

    def forward(i, k):
        src = outs[i] if k == 1 else outs[i].at[1]
        dst = pools[i].at[pl.ds(frames, 2)] if k == 1 else pools[i].at[frames + k]
        return pltpu.make_async_remote_copy(
            src_ref=src, dst_ref=dst, send_sem=fsend.at[i, k - 1], recv_sem=frecv.at[i, k - 1],
            device_id=(jnp.minimum(me + k, n - 1),), device_id_type=MESH,
        )

    def backward(i, k):
        src = gouts[i] if k == 1 else gouts[i].at[1]
        dst = gins[i].at[pl.ds(0, 2)] if k == 1 else gins[i].at[k]
        return pltpu.make_async_remote_copy(
            src_ref=src, dst_ref=dst, send_sem=bsend.at[i, k - 1], recv_sem=brecv.at[i, k - 1],
            device_id=(jnp.maximum(me - k, 0),), device_id_type=MESH,
        )

    for i in range(count):
        for k in range(1, reach + 1):
            @pl.when(me + k < n)
            def _():
                forward(i, k).start()

    for i, (lo, w) in enumerate(groups):
        for f in range(frames):
            pools[i][f, 0] = k_ref[f, :, lo : lo + w]
            pools[i][f, 1] = v_ref[f, :, lo : lo + w]

    contract = lambda a, b, ca, cb: lax.dot_general(
        a, b, (((ca,), (cb,)), ((), ())), preferred_element_type=jnp.float32
    )

    for i, (lo, w) in enumerate(groups):
        cols = slice(lo, lo + w)
        heads = w // head
        lane = lax.broadcasted_iota(jnp.int32, (tokens, w), 1)
        inside = [jnp.logical_and(lane >= h * head, lane < (h + 1) * head) for h in range(heads)]
        keep = [m.astype(jnp.float32).astype(jnp.bfloat16) for m in inside]

        def stacked(x):
            return jnp.concatenate([x * keep[h] for h in range(heads)], axis=0)

        def unstacked(x):
            total = x[:tokens]
            for h in range(1, heads):
                total = jnp.where(inside[h], x[h * tokens : (h + 1) * tokens], total)
            return total

        for k in range(1, reach + 1):
            @pl.when(me >= k)
            def _():
                forward(i, k).wait_recv()

        sum_k, sum_v = [None] * frames, [None] * frames
        out_k = out_v = None

        def add(total, term):
            return term if total is None else total + term

        for f in range(frames):
            qs, gs = stacked(q_ref[f, :, cols]), stacked(g_ref[f, :, cols])
            own, prev = pools[i][owner_slot[f]], pools[i][prev_slot[f]]
            kcat = jnp.concatenate([own[0], prev[0]], axis=0)
            vcat = jnp.concatenate([own[1], prev[1]], axis=0)
            s = contract(kcat, qs, 1, 1) * scale
            dp = contract(vcat, gs, 1, 1)
            e = jnp.exp(s - jnp.max(s, axis=0, keepdims=True))
            p = e * (1.0 / jnp.sum(e, axis=0, keepdims=True))
            ds = p * (dp - jnp.sum(p * dp, axis=0, keepdims=True)) * scale
            p_low, ds_low = p.astype(jnp.bfloat16), ds.astype(jnp.bfloat16)
            att_ref[f, :, cols] = unstacked(contract(p_low, vcat, 0, 0)).astype(jnp.bfloat16)
            gq_ref[f, :, cols] = unstacked(contract(ds_low, kcat, 0, 0)).astype(jnp.bfloat16)
            dv = contract(p_low, gs, 1, 0)
            dk = contract(ds_low, qs, 1, 0)
            for t in range(f + 1):
                here = local[f] == t
                sum_k[t] = add(sum_k[t], jnp.where(here, dk[:tokens], 0.0))
                sum_v[t] = add(sum_v[t], jnp.where(here, dv[:tokens], 0.0))
            remote = local[f] < 0
            out_k = add(out_k, jnp.where(remote, dk[:tokens], 0.0))
            out_v = add(out_v, jnp.where(remote, dv[:tokens], 0.0))
            sum_k[f] = sum_k[f] + jnp.where(opening[f], dk[tokens:], 0.0)
            sum_v[f] = sum_v[f] + jnp.where(opening[f], dv[tokens:], 0.0)
            if f:
                sum_k[f - 1] = sum_k[f - 1] + jnp.where(opening[f], 0.0, dk[tokens:])
                sum_v[f - 1] = sum_v[f - 1] + jnp.where(opening[f], 0.0, dv[tokens:])
            else:
                gouts[i][0, 0] = dk[tokens:].astype(jnp.bfloat16)
                gouts[i][0, 1] = dv[tokens:].astype(jnp.bfloat16)
        gouts[i][1, 0] = out_k.astype(jnp.bfloat16)
        gouts[i][1, 1] = out_v.astype(jnp.bfloat16)
        for k in range(1, reach + 1):
            @pl.when(me >= k)
            def _():
                backward(i, k).start()
        for t in range(frames):
            acc_k[t, :, cols] = sum_k[t]
            acc_v[t, :, cols] = sum_v[t]

    for i, (lo, w) in enumerate(groups):
        cols = slice(lo, lo + w)
        for k in range(1, reach + 1):
            @pl.when(me + k < n)
            def _():
                backward(i, k).wait_recv()
        for part, (acc, result) in enumerate(((acc_k, gk_ref), (acc_v, gv_ref))):
            total = None
            for k in range(1, reach + 1):
                term = jnp.where(returns[k - 1], gins[i][k, part].astype(jnp.float32), 0.0)
                total = term if total is None else total + term
            for t in range(frames):
                value = acc[t, :, cols]
                here = jnp.logical_and(has_start, last_open == t)
                value = value + jnp.where(here, total, 0.0)
                if t == frames - 1:
                    edge = gins[i][0, part].astype(jnp.float32)
                    value = value + jnp.where(next_prev, edge, 0.0)
                result[t, :, cols] = value.astype(jnp.bfloat16)

    for i in range(count):
        for k in range(1, reach + 1):
            @pl.when(me + k < n)
            def _():
                forward(i, k).wait_send()

            @pl.when(me >= k)
            def _():
                backward(i, k).wait_send()


def body(n, queries, keys, values, out_grad, clip_lengths):
    frames, tokens, width = queries.shape
    head = width // HEADS
    reach = min(n - 1, -(-(MAXCLIP - 1) // frames))
    groups = lane_groups(width, head)
    half = jnp.bfloat16
    scratch = [pltpu.VMEM((frames, tokens, width), jnp.float32)] * 2
    scratch += [pltpu.SemaphoreType.DMA((len(groups), reach))] * 4
    scratch += [pltpu.VMEM((2, 2, tokens, w), half) for _, w in groups]
    scratch += [pltpu.VMEM((frames + 1 + reach, 2, tokens, w), half) for _, w in groups]
    scratch += [pltpu.VMEM((2, 2, tokens, w), half) for _, w in groups]
    scratch += [pltpu.VMEM((1 + reach, 2, tokens, w), half) for _, w in groups]
    vmem = pl.BlockSpec(memory_space=pltpu.VMEM)
    return pl.pallas_call(
        functools.partial(kernel, n, reach, groups, head),
        out_shape=[jax.ShapeDtypeStruct(queries.shape, half)] * 4,
        in_specs=[pl.BlockSpec(memory_space=pltpu.SMEM)] + [vmem] * 4,
        out_specs=[vmem] * 4,
        scratch_shapes=scratch,
        compiler_params=pltpu.CompilerParams(
            collective_id=0, has_side_effects=True, vmem_limit_bytes=48 * 1024 * 1024
        ),
    )(clip_lengths, queries, keys, values, out_grad)


def solution(mesh):
    split = P("tm", None, None)
    return jax.shard_map(
        functools.partial(body, mesh.shape["tm"]),
        mesh=mesh,
        in_specs=(split,) * 4 + (P(),),
        out_specs=(split,) * 4,
        check_vma=False,
    )
```

time: 157 us -> 31.3 us (0.20); the launches traced: 153 us -> 30.9 us
  starting transfers between devices: 79.3 us -> 0 us
  matrix products: 26.4 us -> 0 us
  Pallas kernels: 0 us -> 23.2 us
  waiting for transfers between devices: 13.7 us -> 0 us
  other arithmetic: 9.53 us -> 0 us
  local copies, waits for them, and re-layouts: 16.4 us -> 6.98 us
  between operations: 8.11 us -> 0.65 us
    ppermute x26 -> x0, starting transfers between devices: 79.3 us -> none  [from_behind(): lax.ppermute(value, axis, [(source, source + steps) for source in range(i...]
    dot_general x24 -> x0, matrix products: 26.4 us -> none  [the longest x4 8.73 us: attend_frame(): jnp.einsum('hqk,qhd->khd', score_low, query_heads, preferred_element_type...]
    pallas_call x0 -> x1, Pallas kernels: none -> 23.2 us  [body(): pl.pallas_call(functools.partial(kernel, n, reach, groups, head), out_sha...]
    ppermute x26 -> x0, waiting for transfers between devices: 13.7 us -> none  [from_behind(): lax.ppermute(value, axis, [(source, source + steps) for source in range(i...]
    sub x5 -> x0, other arithmetic: 3.93 us -> none  [the longest x4 3.27 us: attend_frame(): expos = jnp.exp(scores - row_max)]
    unnamed x54 -> x14, local copies, waits for them, and re-layouts: 3.9 us -> 6.98 us
    another operation x17 -> x0, local copies, waits for them, and re-layouts: 3.06 us -> none
    concatenate x24 -> x0, local copies, waits for them, and re-layouts: 2.49 us -> none  [the longest x12 1.24 us: body(): jnp.concatenate([value_frames[position], prev_values[position]], axis=0)]
  transfers between devices with their start and end apart: 26 -> 0, of which waited for: 11 -> 0; matrix products, arithmetic and copies ran while one was open for 7% -> 0% of each run, Pallas kernels for 0% -> 0%
where the time goes in v1:
time: 31.3 us; the launch traced here: 30.9 us
  Pallas kernels  23.2 us (74%)
  local copies, waits for them, and re-layouts  6.98 us (22%)
  between operations  0.65 us (2%)
    pallas_call x1, Pallas kernels, body(): pl.pallas_call(functools.partial(kernel, n, reach, groups, head), out_sha...  23.2 us
    unnamed x14, local copies, waits for them, and re-layouts  6.98 us

profile of v1, /device:TPU:19, one launch (start us, length us, event | category | flops | bytes accessed | tf_op | source)
XLA Modules:
  0.0 30.9 jit_solution(10231830171032992686)
XLA Ops:
  0.6 0.0 copy-start
  0.6 0.9 %copy-done = bf16[4,32,640]{2,1,0:T(8,128)(2,1)S(1)} copy-done((bf16[4,32,640]{2,1,0:T(8,128)(2,1)S(1)}, bf16[4,32,640]{2,1,0:T(8,128)(2,1)}, u32[]{:S(2)}) %copy-start) | copy-done | bytes 163864
  1.5 0.0 copy-start.1
  1.6 0.9 %copy-done.1 = bf16[4,32,640]{2,1,0:T(8,128)(2,1)S(1)} copy-done((bf16[4,32,640]{2,1,0:T(8,128)(2,1)S(1)}, bf16[4,32,640]{2,1,0:T(8,128)(2,1)}, u32[]{:S(2)}) %copy-start.1) | copy-done | bytes 163864
  2.5 0.0 copy-start.2
  2.5 0.9 %copy-done.2 = bf16[4,32,640]{2,1,0:T(8,128)(2,1)S(1)} copy-done((bf16[4,32,640]{2,1,0:T(8,128)(2,1)S(1)}, bf16[4,32,640]{2,1,0:T(8,128)(2,1)}, u32[]{:S(2)}) %copy-start.2) | copy-done | bytes 163864
  3.4 0.0 copy-start.3
  3.4 0.9 %copy-done.3 = bf16[4,32,640]{2,1,0:T(8,128)(2,1)S(1)} copy-done((bf16[4,32,640]{2,1,0:T(8,128)(2,1)S(1)}, bf16[4,32,640]{2,1,0:T(8,128)(2,1)}, u32[]{:S(2)}) %copy-start.3) | copy-done | bytes 163864
  4.3 0.0 copy-start.4
  4.3 0.7 %copy-done.4 = s32[16]{0:T(128)S(1)} copy-done((s32[16]{0:T(128)S(1)}, s32[16]{0:T(128)}, u32[]{:S(2)}) %copy-start.4) | copy-done | bytes 88
  5.0 23.2 %shard_map.84 = (bf16[4,32,640]{2,1,0:T(8,128)(2,1)S(1)}, bf16[4,32,640]{2,1,0:T(8,128)(2,1)S(1)}, bf16[4,32,640]{2,1,0:T(8,128)(2,1)S(1)}, bf16[4,32,640]{2,1,0:T(8,128)(2,1)S(1)}) custom-call(s32[16]{0:T(128)S(1)} %copy-done.4, bf16[4,32,640]{2,1,0:T(8,128)(2,1)S(1)} %copy-done, bf16[4,32,640]{2,1,0:T(8,128)(2,1)S(1)} %copy-done.1, ...), custom_call_target="tpu_custom_call" | custom-call | tf_op jit(solution)/shard_map/pallas_call | solution.py:222
  28.2 0.7 %copy.13 = bf16[4,32,640]{2,1,0:T(8,128)(2,1)} copy(bf16[4,32,640]{2,1,0:T(8,128)(2,1)S(1)} %get-tuple-element.8) | data formatting | bytes 327680
  28.9 0.7 %copy.14 = bf16[4,32,640]{2,1,0:T(8,128)(2,1)} copy(bf16[4,32,640]{2,1,0:T(8,128)(2,1)S(1)} %get-tuple-element.9) | data formatting | bytes 327680
  29.5 0.7 %copy.15 = bf16[4,32,640]{2,1,0:T(8,128)(2,1)} copy(bf16[4,32,640]{2,1,0:T(8,128)(2,1)S(1)} %get-tuple-element.10) | data formatting | bytes 327680
  30.2 0.7 %copy.16 = bf16[4,32,640]{2,1,0:T(8,128)(2,1)} copy(bf16[4,32,640]{2,1,0:T(8,128)(2,1)S(1)} %get-tuple-element.11) | data formatting | bytes 327680
Async XLA Ops:
  0.6 0.9 %copy-start = (bf16[4,32,640]{2,1,0:T(8,128)(2,1)S(1)}, bf16[4,32,640]{2,1,0:T(8,128)(2,1)}, u32[]{:S(2)}) copy-start(bf16[4,32,640]{2,1,0:T(8,128)(2,1)} %q_ref.1) | copy-start | bytes 491524
  1.5 0.9 %copy-start.1 = (bf16[4,32,640]{2,1,0:T(8,128)(2,1)S(1)}, bf16[4,32,640]{2,1,0:T(8,128)(2,1)}, u32[]{:S(2)}) copy-start(bf16[4,32,640]{2,1,0:T(8,128)(2,1)} %k_ref.1) | copy-start | bytes 491524
  2.5 0.9 %copy-start.2 = (bf16[4,32,640]{2,1,0:T(8,128)(2,1)S(1)}, bf16[4,32,640]{2,1,0:T(8,128)(2,1)}, u32[]{:S(2)}) copy-start(bf16[4,32,640]{2,1,0:T(8,128)(2,1)} %v_ref.1) | copy-start | bytes 491524
  3.4 0.9 %copy-start.3 = (bf16[4,32,640]{2,1,0:T(8,128)(2,1)S(1)}, bf16[4,32,640]{2,1,0:T(8,128)(2,1)}, u32[]{:S(2)}) copy-start(bf16[4,32,640]{2,1,0:T(8,128)(2,1)} %g_ref.1) | copy-start | bytes 491524
  4.3 0.7 %copy-start.4 = (s32[16]{0:T(128)S(1)}, s32[16]{0:T(128)}, u32[]{:S(2)}) copy-start(s32[16]{0:T(128)} %len_ref.1) | copy-start | bytes 196

commit v2 on v1

v2 whole, which is shorter than its diff:
```python
import functools

import jax
import jax.numpy as jnp
from jax import lax
from jax.experimental import pallas as pl
from jax.experimental.pallas import tpu as pltpu
from jax.sharding import PartitionSpec as P

HEADS = 10
MAXCLIP = 24
MESH = pl.DeviceIdType.MESH


def lane_groups(width, head):
    step = max(256, head)
    return [(start, min(step, width - start)) for start in range(0, width, step)]


def kernel(
    n, reach, groups, head,
    len_ref, q_ref, k_ref, v_ref, g_ref,
    att_ref, gq_ref, gk_ref, gv_ref,
    lens, q_all, g_all, acc_k, acc_v, lsem, fsend, frecv, bsend, brecv, *bufs,
):
    count = len(groups)
    bufs = [bufs[j * count : (j + 1) * count] for j in range(len(bufs) // count)]
    starts, pools, chip_out, chip_in, qst, gst, gouts, gins, gchip_out, gchip_in, gtots = bufs
    frames, tokens, _ = q_ref.shape
    me = lax.axis_index("tm")
    core = lax.rem(me, 2)
    chip = lax.div(me, 2)
    chips = n // 2
    sibling = me + 1 - 2 * core
    scale = head ** (-0.5)
    edge, near, far = frames, frames + 1, frames + 2
    half = jnp.bfloat16

    loads = [pltpu.make_async_copy(len_ref, lens, lsem.at[0])]
    for i, (lo, w) in enumerate(groups):
        for part, ref in enumerate((k_ref, v_ref)):
            loads.append(pltpu.make_async_copy(
                ref.at[:, :, pl.ds(lo, w)], pools[i].at[pl.ds(0, frames), part],
                lsem.at[1 + 2 * i + part],
            ))
    late = [
        pltpu.make_async_copy(q_ref, q_all, lsem.at[1 + 2 * count]),
        pltpu.make_async_copy(g_ref, g_all, lsem.at[2 + 2 * count]),
    ]
    for copy in loads + late:
        copy.start()

    barrier = pltpu.get_barrier_semaphore()

    def greet(device):
        pl.semaphore_signal(barrier, inc=1, device_id=(device,), device_id_type=MESH)

    greet(sibling)
    for k in range(1, reach + 1):
        @pl.when(chip + k < chips)
        def _():
            greet(me + 2 * k)

        @pl.when(chip >= k)
        def _():
            greet(me - 2 * k)

    @pl.when(jnp.logical_and(core == 1, me + 1 < n))
    def _():
        greet(me + 1)

    @pl.when(jnp.logical_and(core == 0, me > 0))
    def _():
        greet(me - 1)

    greeted = 1 + jnp.minimum(reach, chips - 1 - chip) + jnp.minimum(reach, chip)
    greeted += jnp.where(core == 1, jnp.minimum(1, n - 1 - me), jnp.minimum(1, me))

    first = me * frames
    chip_first = chip * (2 * frames)
    wanted = [first + f for f in range(frames)]
    wanted += [chip_first, chip_first + frames, chip_first + 2 * frames - 1]
    wanted += [chip_first + k * 2 * frames for k in range(1, reach + 1)]
    loads[0].wait()

    def scan_clips(c, carry):
        start, owners = carry
        owners = tuple(jnp.where(start <= w, start, o) for w, o in zip(wanted, owners))
        return start + lens[c], owners

    zero = jnp.int32(0)
    _, owners = lax.fori_loop(0, len_ref.shape[0], scan_clips, (zero, (zero,) * len(wanted)))
    own_first, own_mid, own_last = owners[frames : frames + 3]
    own_later = owners[frames + 3 :]
    local = [owners[f] - first for f in range(frames)]
    opening = [local[f] == f for f in range(frames)]
    last_open = jnp.clip(local[frames - 1], 0, frames - 1)
    back = jnp.clip(chip - lax.div(own_first, jnp.int32(2 * frames)), 1, reach)
    away = [
        jnp.where(jnp.logical_and(core == 1, owners[f] >= chip_first), near, far)
        for f in range(frames)
    ]
    owner_slot = [jnp.where(local[f] >= 0, local[f], away[f]) for f in range(frames)]
    prev_slot = [jnp.where(opening[f], f, f - 1 if f else edge) for f in range(frames)]
    last_in_core1 = own_last >= chip_first + frames
    mid_outside = own_mid < chip_first
    mid_in_core0 = jnp.logical_and(
        core == 0, jnp.logical_and(own_mid >= chip_first, own_mid < chip_first + frames)
    )
    returns = [
        jnp.logical_and(
            chip + k < chips,
            jnp.logical_and(own_later[k - 1] >= chip_first, own_later[k - 1] < chip_first + 2 * frames),
        )
        for k in range(1, reach + 1)
    ]
    holder = jnp.logical_and(own_last >= first, own_last < first + frames)
    next_first = jnp.where(core == 0, own_mid, own_later[0])
    next_prev = jnp.logical_and(next_first != first + frames, me + 1 < n)

    def remote(src, dst, send, recv, i, slot, device):
        return pltpu.make_async_remote_copy(
            src_ref=src, dst_ref=dst, send_sem=send.at[i, slot], recv_sem=recv.at[i, slot],
            device_id=(device,), device_id_type=MESH,
        )

    after, before = jnp.minimum(me + 1, n - 1), jnp.maximum(me - 1, 0)
    fwd_edge = lambda i: remote(
        pools[i].at[frames - 1], pools[i].at[edge], fsend, frecv, i, 0, after)
    fwd_near0 = lambda i: remote(starts[i], pools[i].at[near], fsend, frecv, i, 1, sibling)
    fwd_near1 = lambda i: remote(
        starts[i].at[0], pools[i].at[near, 0], fsend, frecv, i, 1, sibling)
    fwd_far = lambda i: remote(
        pools[i].at[far, core], pools[i].at[far, core], fsend, frecv, i, 2, sibling)
    fwd_far_in = lambda i: remote(
        pools[i].at[far, core], pools[i].at[far, 1 - core], fsend, frecv, i, 2, sibling)
    fwd_chip = lambda i, k: remote(
        chip_out[i], chip_in[i].at[k - 1], fsend, frecv, i, 2 + k, jnp.minimum(me + 2 * k, n - 1))
    bwd_edge = lambda i: remote(gouts[i].at[0], gins[i].at[0], bsend, brecv, i, 0, before)
    bwd_near1 = lambda i: remote(gouts[i].at[1], gins[i].at[1], bsend, brecv, i, 1, sibling)
    bwd_near0 = lambda i: remote(
        gouts[i].at[1, 1], gins[i].at[1, 1], bsend, brecv, i, 1, sibling)
    bwd_tot = lambda i: remote(
        gtots[i].at[core], gtots[i].at[core], bsend, brecv, i, 2, sibling)
    bwd_tot_in = lambda i: remote(
        gtots[i].at[core], gtots[i].at[1 - core], bsend, brecv, i, 2, sibling)
    bwd_chip = lambda i, k: remote(
        gchip_out[i], gchip_in[i].at[k - 1], bsend, brecv, i, 2 + k, jnp.maximum(me - 2 * k, 0))

    def when(condition, act):
        @pl.when(condition)
        def _():
            act()

    for copy in loads[1:]:
        copy.wait()
    for i in range(count):
        start = pools[i][0]
        for f in range(1, frames):
            start = jnp.where(last_open == f, pools[i][f], start)
        starts[i][...] = start
    pl.semaphore_wait(barrier, greeted)

    for i in range(count):
        when(core == 0, lambda: fwd_near0(i).start())
        when(core == 1, lambda: fwd_near1(i).start())
    for i in range(count):
        when(me + 1 < n, lambda: fwd_edge(i).start())

    for i in range(count):
        when(core == 1, lambda: fwd_near0(i).wait_recv())
        when(core == 0, lambda: fwd_near1(i).wait_recv())
        own, other = starts[i][core], pools[i][near, core]
        take_own = jnp.where(core == 1, last_in_core1, jnp.logical_not(last_in_core1))
        chip_out[i][...] = jnp.where(take_own, own, other)
        for k in range(1, reach + 1):
            when(chip + k < chips, lambda: fwd_chip(i, k).start())

    for copy in late:
        copy.wait()

    def masks(w):
        lane = lax.broadcasted_iota(jnp.int32, (tokens, w), 1)
        return [
            jnp.logical_and(lane >= h * head, lane < (h + 1) * head) for h in range(w // head)
        ]

    for i, (lo, w) in enumerate(groups):
        keep = [m.astype(jnp.float32).astype(half) for m in masks(w)]
        for f in range(frames):
            for h, m in enumerate(keep):
                rows = slice(h * tokens, (h + 1) * tokens)
                qst[i][f, rows] = q_all[f, :, lo : lo + w] * m
                gst[i][f, rows] = g_all[f, :, lo : lo + w] * m

    def contract(a, b, ca, cb):
        return lax.dot_general(
            a, b, (((ca,), (cb,)), ((), ())), preferred_element_type=jnp.float32
        )

    def relay(i):
        for k in range(1, reach + 1):
            when(chip >= k, lambda: fwd_chip(i, k).wait_recv())
        pools[i][far, core] = chip_in[i][back - 1]
        fwd_far(i).start()

    def compute(i):
        lo, w = groups[i]
        cols = slice(lo, lo + w)
        inside = masks(w)

        def unstacked(x):
            total = x[:tokens]
            for h in range(1, w // head):
                total = jnp.where(inside[h], x[h * tokens : (h + 1) * tokens], total)
            return total.astype(half)

        each = range(frames)
        own = [pools[i][owner_slot[f]] for f in each]
        prev = [pools[i][prev_slot[f]] for f in each]
        kcat = [jnp.concatenate([own[f][0], prev[f][0]], axis=0) for f in each]
        vcat = [jnp.concatenate([own[f][1], prev[f][1]], axis=0) for f in each]
        s = [contract(kcat[f], qst[i][f], 1, 1) * scale for f in each]
        dp = [contract(vcat[f], gst[i][f], 1, 1) for f in each]
        e = [jnp.exp(s[f] - jnp.max(s[f], axis=0, keepdims=True)) for f in each]
        p = [e[f] * (1.0 / jnp.sum(e[f], axis=0, keepdims=True)) for f in each]
        p_low = [p[f].astype(half) for f in each]
        ds = [p[f] * (dp[f] - jnp.sum(p[f] * dp[f], axis=0, keepdims=True)) * scale for f in each]
        ds_low = [ds[f].astype(half) for f in each]
        dv = [contract(p_low[f], gst[i][f], 1, 0) for f in each]
        dk = [contract(ds_low[f], qst[i][f], 1, 0) for f in each]
        for part, (d, acc) in enumerate(((dk, acc_k), (dv, acc_v))):
            gouts[i][0, part] = d[0][tokens:].astype(half)
            out = jnp.zeros((tokens, w), jnp.float32)
            for f in each:
                out = out + jnp.where(local[f] < 0, d[f][:tokens], 0.0)
            gouts[i][1, part] = out.astype(half)
            for t in each:
                total = jnp.where(opening[t], d[t][tokens:], 0.0)
                if t + 1 < frames:
                    total = total + jnp.where(opening[t + 1], 0.0, d[t + 1][tokens:])
                for f in range(t, frames):
                    total = total + jnp.where(local[f] == t, d[f][:tokens], 0.0)
                acc[t, :, cols] = total
        when(core == 1, lambda: bwd_near1(i).start())
        when(core == 0, lambda: bwd_near0(i).start())
        when(me > 0, lambda: bwd_edge(i).start())
        for f in each:
            att_ref[f, :, cols] = unstacked(contract(p_low[f], vcat[f], 0, 0))
            gq_ref[f, :, cols] = unstacked(contract(ds_low[f], kcat[f], 0, 0))

    def chip_sum(i):
        when(core == 0, lambda: bwd_near1(i).wait_recv())
        when(core == 1, lambda: bwd_near0(i).wait_recv())
        mine = gouts[i][1, core].astype(jnp.float32)
        other = gins[i][1, core].astype(jnp.float32)
        keep_mine = jnp.logical_or(core == 0, mid_outside)
        keep_other = jnp.logical_or(core == 1, mid_outside)
        both = jnp.where(keep_mine, mine, 0.0) + jnp.where(keep_other, other, 0.0)
        gchip_out[i][...] = both.astype(half)
        for k in range(1, reach + 1):
            when(chip >= k, lambda: bwd_chip(i, k).start())

    def returned(i):
        for k in range(1, reach + 1):
            when(chip + k < chips, lambda: bwd_chip(i, k).wait_recv())
        total = None
        for k in range(1, reach + 1):
            term = jnp.where(returns[k - 1], gchip_in[i][k - 1].astype(jnp.float32), 0.0)
            total = term if total is None else total + term
        gtots[i][core] = total.astype(half)
        bwd_tot(i).start()

    def finish(i):
        lo, w = groups[i]
        cols = slice(lo, lo + w)
        when(me + 1 < n, lambda: bwd_edge(i).wait_recv())
        bwd_tot_in(i).wait_recv()
        for part, (acc, result) in enumerate(((acc_k, gk_ref), (acc_v, gv_ref))):
            total = jnp.where(holder, gtots[i][part].astype(jnp.float32), 0.0)
            total = total + jnp.where(mid_in_core0, gins[i][1, part].astype(jnp.float32), 0.0)
            for t in range(frames):
                value = acc[t, :, cols] + jnp.where(last_open == t, total, 0.0)
                if t == frames - 1:
                    behind = gins[i][0, part].astype(jnp.float32)
                    value = value + jnp.where(next_prev, behind, 0.0)
                result[t, :, cols] = value.astype(half)

    relay(0)
    for i in range(count):
        if i + 1 < count:
            relay(i + 1)
        fwd_far_in(i).wait_recv()
        when(me > 0, lambda: fwd_edge(i).wait_recv())
        compute(i)
        if i:
            chip_sum(i - 1)
    chip_sum(count - 1)
    for i in range(count):
        returned(i)
    for i in range(count):
        finish(i)

    for i in range(count):
        when(core == 0, lambda: fwd_near0(i).wait_send())
        when(core == 1, lambda: fwd_near1(i).wait_send())
        when(core == 0, lambda: bwd_near0(i).wait_send())
        when(core == 1, lambda: bwd_near1(i).wait_send())
        when(me + 1 < n, lambda: fwd_edge(i).wait_send())
        when(me > 0, lambda: bwd_edge(i).wait_send())
        fwd_far(i).wait_send()
        bwd_tot(i).wait_send()
        for k in range(1, reach + 1):
            when(chip + k < chips, lambda: fwd_chip(i, k).wait_send())
            when(chip >= k, lambda: bwd_chip(i, k).wait_send())


def store_kernel(*refs):
    count = len(refs) // 2
    sems = refs[-1]
    copies = [
        pltpu.make_async_copy(refs[j], refs[count + j], sems.at[j]) for j in range(count)
    ]
    for copy in copies:
        copy.start()
    for copy in copies:
        copy.wait()


def body(n, queries, keys, values, out_grad, clip_lengths):
    frames, tokens, width = queries.shape
    head = width // HEADS
    reach = min(n // 2 - 1, -(-(MAXCLIP - 1) // (2 * frames)))
    groups = lane_groups(width, head)
    count = len(groups)
    half = jnp.bfloat16
    scratch = [pltpu.SMEM(clip_lengths.shape, jnp.int32)]
    scratch += [pltpu.VMEM((frames, tokens, width), half)] * 2
    scratch += [pltpu.VMEM((frames, tokens, width), jnp.float32)] * 2
    scratch += [pltpu.SemaphoreType.DMA((3 + 2 * count,))]
    scratch += [pltpu.SemaphoreType.DMA((count, 3 + reach))] * 4
    shapes = [
        lambda w: (2, tokens, w),
        lambda w: (frames + 3, 2, tokens, w),
        lambda w: (tokens, w),
        lambda w: (reach, tokens, w),
        lambda w: (frames, w // head * tokens, w),
        lambda w: (frames, w // head * tokens, w),
        lambda w: (2, 2, tokens, w),
        lambda w: (2, 2, tokens, w),
        lambda w: (tokens, w),
        lambda w: (reach, tokens, w),
        lambda w: (2, tokens, w),
    ]
    scratch += [pltpu.VMEM(shape(w), half) for shape in shapes for _, w in groups]
    vmem = pl.BlockSpec(memory_space=pltpu.VMEM)
    hbm = pl.BlockSpec(memory_space=pltpu.HBM)
    like = [jax.ShapeDtypeStruct(queries.shape, half)] * 4
    args = (clip_lengths, queries, keys, values, out_grad)
    results = pl.pallas_call(
        functools.partial(kernel, n, reach, groups, head),
        out_shape=like,
        in_specs=[hbm] * 5,
        out_specs=[vmem] * 4,
        scratch_shapes=scratch,
        compiler_params=pltpu.CompilerParams(
            collective_id=0, has_side_effects=True, vmem_limit_bytes=48 * 1024 * 1024
        ),
    )(*[pltpu.with_memory_space_constraint(a, pltpu.HBM) for a in args])
    return pl.pallas_call(
        store_kernel,
        out_shape=like,
        in_specs=[vmem] * 4,
        out_specs=[hbm] * 4,
        scratch_shapes=[pltpu.SemaphoreType.DMA((4,))],
    )(*results)


def solution(mesh):
    split = P("tm", None, None)
    return jax.shard_map(
        functools.partial(body, mesh.shape["tm"]),
        mesh=mesh,
        in_specs=(split,) * 4 + (P(),),
        out_specs=(split,) * 4,
        check_vma=False,
    )
```

time: 31.3 us -> 22.7 us (0.73)
  local copies, waits for them, and re-layouts: 6.98 us -> 2.63 us
  Pallas kernels: 23.2 us -> 19.2 us
    pallas_call x1, Pallas kernels: 23.2 us -> 17.2 us  [body(): pl.pallas_call(functools.partial(kernel, n, reach, groups, head), out_sha...]
    unnamed x14 -> x8, local copies, waits for them, and re-layouts: 6.98 us -> 2.63 us
    pallas_call x0 -> x1, Pallas kernels: none -> 2.01 us  [body(): pl.pallas_call(store_kernel, out_shape=like, in_specs=[vmem] * 4, out_spe...]
where the time goes in v2:
time: 22.7 us; the launch traced here: 22.5 us
  Pallas kernels  19.2 us (85%)
  local copies, waits for them, and re-layouts  2.63 us (12%)
  between operations  0.65 us (3%)
    pallas_call x1, Pallas kernels, body(): pl.pallas_call(functools.partial(kernel, n, reach, groups, head), out_sha...  17.2 us
    unnamed x8, local copies, waits for them, and re-layouts  2.63 us
    pallas_call x1, Pallas kernels, body(): pl.pallas_call(store_kernel, out_shape=like, in_specs=[vmem] * 4, out_spe...  2.01 us

profile of v2, /device:TPU:19, one launch (start us, length us, event | category | flops | bytes accessed | tf_op | source)
XLA Modules:
  0.0 22.5 jit_solution(13873369527209741778)
XLA Ops:
  0.6 17.2 %shard_map.84 = (bf16[4,32,640]{2,1,0:T(8,128)(2,1)S(1)}, bf16[4,32,640]{2,1,0:T(8,128)(2,1)S(1)}, bf16[4,32,640]{2,1,0:T(8,128)(2,1)S(1)}, bf16[4,32,640]{2,1,0:T(8,128)(2,1)S(1)}) custom-call(s32[16]{0:T(128)} %len_ref.1, bf16[4,32,640]{2,1,0:T(8,128)(2,1)} %q_ref.1, bf16[4,32,640]{2,1,0:T(8,128)(2,1)} %k_ref.1, bf16[4,32,640]{2,1,0:T(8,128)(2,1)} %v_ref.1, ...), custom_call_target="tpu_custom_call" | custom-call | tf_op jit(solution)/shard_map/pallas_call | solution.py:360
  17.8 0.0 copy-start
  17.9 0.6 %copy-done = bf16[4,32,640]{2,1,0:T(8,128)(2,1)} copy-done((bf16[4,32,640]{2,1,0:T(8,128)(2,1)}, bf16[4,32,640]{2,1,0:T(8,128)(2,1)S(1)}, u32[]{:S(2)}) %copy-start) | copy-done | bytes 163864
  18.5 0.0 copy-start.1
  18.5 0.7 %copy-done.1 = bf16[4,32,640]{2,1,0:T(8,128)(2,1)} copy-done((bf16[4,32,640]{2,1,0:T(8,128)(2,1)}, bf16[4,32,640]{2,1,0:T(8,128)(2,1)S(1)}, u32[]{:S(2)}) %copy-start.1) | copy-done | bytes 163864
  19.2 0.0 copy-start.2
  19.2 0.7 %copy-done.2 = bf16[4,32,640]{2,1,0:T(8,128)(2,1)} copy-done((bf16[4,32,640]{2,1,0:T(8,128)(2,1)}, bf16[4,32,640]{2,1,0:T(8,128)(2,1)S(1)}, u32[]{:S(2)}) %copy-start.2) | copy-done | bytes 163864
  19.8 0.0 copy-start.3
  19.8 0.7 %copy-done.3 = bf16[4,32,640]{2,1,0:T(8,128)(2,1)} copy-done((bf16[4,32,640]{2,1,0:T(8,128)(2,1)}, bf16[4,32,640]{2,1,0:T(8,128)(2,1)S(1)}, u32[]{:S(2)}) %copy-start.3) | copy-done | bytes 163864
  20.5 2.0 %shard_map.85 = (bf16[4,32,640]{2,1,0:T(8,128)(2,1)}, bf16[4,32,640]{2,1,0:T(8,128)(2,1)}, bf16[4,32,640]{2,1,0:T(8,128)(2,1)}, bf16[4,32,640]{2,1,0:T(8,128)(2,1)}) custom-call(bf16[4,32,640]{2,1,0:T(8,128)(2,1)} %copy-done, bf16[4,32,640]{2,1,0:T(8,128)(2,1)} %copy-done.1, bf16[4,32,640]{2,1,0:T(8,128)(2,1)} %copy-done.2, bf16[4,32,640]{2,1,0:T(8,128)(2,1)} %copy-done.3), custom_call_target="tpu_custom_call" | custom-call | tf_op jit(solution)/shard_map/pallas_call | solution.py:370
Async XLA Ops:
  17.8 0.7 %copy-start = (bf16[4,32,640]{2,1,0:T(8,128)(2,1)}, bf16[4,32,640]{2,1,0:T(8,128)(2,1)S(1)}, u32[]{:S(2)}) copy-start(bf16[4,32,640]{2,1,0:T(8,128)(2,1)S(1)} %get-tuple-element.8.refs_0_) | copy-start | bytes 491524
  18.5 0.7 %copy-start.1 = (bf16[4,32,640]{2,1,0:T(8,128)(2,1)}, bf16[4,32,640]{2,1,0:T(8,128)(2,1)S(1)}, u32[]{:S(2)}) copy-start(bf16[4,32,640]{2,1,0:T(8,128)(2,1)S(1)} %get-tuple-element.9.refs_1_) | copy-start | bytes 491524
  19.2 0.7 %copy-start.2 = (bf16[4,32,640]{2,1,0:T(8,128)(2,1)}, bf16[4,32,640]{2,1,0:T(8,128)(2,1)S(1)}, u32[]{:S(2)}) copy-start(bf16[4,32,640]{2,1,0:T(8,128)(2,1)S(1)} %get-tuple-element.10.refs_2_) | copy-start | bytes 491524
  19.8 0.7 %copy-start.3 = (bf16[4,32,640]{2,1,0:T(8,128)(2,1)}, bf16[4,32,640]{2,1,0:T(8,128)(2,1)S(1)}, u32[]{:S(2)}) copy-start(bf16[4,32,640]{2,1,0:T(8,128)(2,1)S(1)} %get-tuple-element.11.refs_3_) | copy-start | bytes 491524

commit v3 on v2

--- a/solution.py
+++ b/solution.py
@@ -21,11 +21,13 @@
     n, reach, groups, head,
     len_ref, q_ref, k_ref, v_ref, g_ref,
     att_ref, gq_ref, gk_ref, gv_ref,
-    lens, q_all, g_all, acc_k, acc_v, lsem, fsend, frecv, bsend, brecv, *bufs,
+    lens, q_all, g_all, acc_k, acc_v, edges, gedge_out, gedge_in,
+    lsem, esend, erecv, fsend, frecv, bsend, brecv, *bufs,
 ):
     count = len(groups)
     bufs = [bufs[j * count : (j + 1) * count] for j in range(len(bufs) // count)]
-    starts, pools, chip_out, chip_in, qst, gst, gouts, gins, gchip_out, gchip_in, gtots = bufs
+    starts, pools, chip_out, chip_in, qst, gst, pst, dst = bufs[:8]
+    gouts, gins, gchip_out, gchip_in, gtots = bufs[8:]
     frames, tokens, _ = q_ref.shape
     me = lax.axis_index("tm")
     core = lax.rem(me, 2)
@@ -33,7 +35,7 @@
     chips = n // 2
     sibling = me + 1 - 2 * core
     scale = head ** (-0.5)
-    edge, near, far = frames, frames + 1, frames + 2
+    near, far = frames, frames + 1
     half = jnp.bfloat16
 
     loads = [pltpu.make_async_copy(len_ref, lens, lsem.at[0])]
@@ -101,7 +103,7 @@
         for f in range(frames)
     ]
     owner_slot = [jnp.where(local[f] >= 0, local[f], away[f]) for f in range(frames)]
-    prev_slot = [jnp.where(opening[f], f, f - 1 if f else edge) for f in range(frames)]
+    prev_slot = [jnp.where(opening[f], f, f - 1) for f in range(1, frames)]
     last_in_core1 = own_last >= chip_first + frames
     mid_outside = own_mid < chip_first
     mid_in_core0 = jnp.logical_and(
@@ -118,34 +120,36 @@
     next_first = jnp.where(core == 0, own_mid, own_later[0])
     next_prev = jnp.logical_and(next_first != first + frames, me + 1 < n)
 
-    def remote(src, dst, send, recv, i, slot, device):
+    def ends(src, dst, send_sem, recv_sem, device):
         return pltpu.make_async_remote_copy(
-            src_ref=src, dst_ref=dst, send_sem=send.at[i, slot], recv_sem=recv.at[i, slot],
+            src_ref=src, dst_ref=dst, send_sem=send_sem, recv_sem=recv_sem,
             device_id=(device,), device_id_type=MESH,
         )
 
+    def remote(src, dst, send, recv, i, slot, device):
+        return ends(src, dst, send.at[i, slot], recv.at[i, slot], device)
+
     after, before = jnp.minimum(me + 1, n - 1), jnp.maximum(me - 1, 0)
-    fwd_edge = lambda i: remote(
-        pools[i].at[frames - 1], pools[i].at[edge], fsend, frecv, i, 0, after)
-    fwd_near0 = lambda i: remote(starts[i], pools[i].at[near], fsend, frecv, i, 1, sibling)
+    fwd_edge = lambda part: ends(
+        (k_ref, v_ref)[part].at[frames - 1], edges.at[part], esend.at[part], erecv.at[part], after)
+    bwd_edge = lambda: ends(gedge_out, gedge_in, esend.at[2], erecv.at[2], before)
+    fwd_near0 = lambda i: remote(starts[i], pools[i].at[near], fsend, frecv, i, 0, sibling)
     fwd_near1 = lambda i: remote(
-        starts[i].at[0], pools[i].at[near, 0], fsend, frecv, i, 1, sibling)
+        starts[i].at[0], pools[i].at[near, 0], fsend, frecv, i, 0, sibling)
     fwd_far = lambda i: remote(
-        pools[i].at[far, core], pools[i].at[far, core], fsend, frecv, i, 2, sibling)
+        pools[i].at[far, core], pools[i].at[far, core], fsend, frecv, i, 1, sibling)
     fwd_far_in = lambda i: remote(
-        pools[i].at[far, core], pools[i].at[far, 1 - core], fsend, frecv, i, 2, sibling)
+        pools[i].at[far, core], pools[i].at[far, 1 - core], fsend, frecv, i, 1, sibling)
     fwd_chip = lambda i, k: remote(
-        chip_out[i], chip_in[i].at[k - 1], fsend, frecv, i, 2 + k, jnp.minimum(me + 2 * k, n - 1))
-    bwd_edge = lambda i: remote(gouts[i].at[0], gins[i].at[0], bsend, brecv, i, 0, before)
-    bwd_near1 = lambda i: remote(gouts[i].at[1], gins[i].at[1], bsend, brecv, i, 1, sibling)
-    bwd_near0 = lambda i: remote(
-        gouts[i].at[1, 1], gins[i].at[1, 1], bsend, brecv, i, 1, sibling)
+        chip_out[i], chip_in[i].at[k - 1], fsend, frecv, i, 1 + k, jnp.minimum(me + 2 * k, n - 1))
+    bwd_near1 = lambda i: remote(gouts[i], gins[i], bsend, brecv, i, 0, sibling)
+    bwd_near0 = lambda i: remote(gouts[i].at[1], gins[i].at[1], bsend, brecv, i, 0, sibling)
     bwd_tot = lambda i: remote(
-        gtots[i].at[core], gtots[i].at[core], bsend, brecv, i, 2, sibling)
+        gtots[i].at[core], gtots[i].at[core], bsend, brecv, i, 1, sibling)
     bwd_tot_in = lambda i: remote(
-        gtots[i].at[core], gtots[i].at[1 - core], bsend, brecv, i, 2, sibling)
+        gtots[i].at[core], gtots[i].at[1 - core], bsend, brecv, i, 1, sibling)
     bwd_chip = lambda i, k: remote(
-        gchip_out[i], gchip_in[i].at[k - 1], bsend, brecv, i, 2 + k, jnp.maximum(me - 2 * k, 0))
+        gchip_out[i], gchip_in[i].at[k - 1], bsend, brecv, i, 1 + k, jnp.maximum(me - 2 * k, 0))
 
     def when(condition, act):
         @pl.when(condition)
@@ -164,8 +168,8 @@
     for i in range(count):
         when(core == 0, lambda: fwd_near0(i).start())
         when(core == 1, lambda: fwd_near1(i).start())
-    for i in range(count):
-        when(me + 1 < n, lambda: fwd_edge(i).start())
+    for part in range(2):
+        when(me + 1 < n, lambda: fwd_edge(part).start())
 
     for i in range(count):
         when(core == 1, lambda: fwd_near0(i).wait_recv())
@@ -204,37 +208,43 @@
         pools[i][far, core] = chip_in[i][back - 1]
         fwd_far(i).start()
 
-    def compute(i):
+    each = range(frames)
+
+    def frame_sets(i):
         lo, w = groups[i]
-        cols = slice(lo, lo + w)
-        inside = masks(w)
-
-        def unstacked(x):
-            total = x[:tokens]
-            for h in range(1, w // head):
-                total = jnp.where(inside[h], x[h * tokens : (h + 1) * tokens], total)
-            return total.astype(half)
-
-        each = range(frames)
         own = [pools[i][owner_slot[f]] for f in each]
-        prev = [pools[i][prev_slot[f]] for f in each]
-        kcat = [jnp.concatenate([own[f][0], prev[f][0]], axis=0) for f in each]
-        vcat = [jnp.concatenate([own[f][1], prev[f][1]], axis=0) for f in each]
+        prev = [jnp.where(opening[0], pools[i][0], edges[:, :, lo : lo + w])]
+        prev += [pools[i][prev_slot[f - 1]] for f in each[1:]]
+        return [
+            [jnp.concatenate([own[f][part], prev[f][part]], axis=0) for f in each]
+            for part in range(2)
+        ]
+
+    def scores(i):
+        kcat, vcat = frame_sets(i)
         s = [contract(kcat[f], qst[i][f], 1, 1) * scale for f in each]
         dp = [contract(vcat[f], gst[i][f], 1, 1) for f in each]
         e = [jnp.exp(s[f] - jnp.max(s[f], axis=0, keepdims=True)) for f in each]
         p = [e[f] * (1.0 / jnp.sum(e[f], axis=0, keepdims=True)) for f in each]
-        p_low = [p[f].astype(half) for f in each]
         ds = [p[f] * (dp[f] - jnp.sum(p[f] * dp[f], axis=0, keepdims=True)) * scale for f in each]
-        ds_low = [ds[f].astype(half) for f in each]
-        dv = [contract(p_low[f], gst[i][f], 1, 0) for f in each]
-        dk = [contract(ds_low[f], qst[i][f], 1, 0) for f in each]
-        for part, (d, acc) in enumerate(((dk, acc_k), (dv, acc_v))):
-            gouts[i][0, part] = d[0][tokens:].astype(half)
+        for f in each:
+            pst[i][f] = p[f].astype(half)
+            dst[i][f] = ds[f].astype(half)
+
+    def key_grads(i):
+        lo, w = groups[i]
+        cols = slice(lo, lo + w)
+        dk = [contract(dst[i][f], qst[i][f], 1, 0) for f in each]
+        dv = [contract(pst[i][f], gst[i][f], 1, 0) for f in each]
+        for part, d in enumerate((dk, dv)):
+            gedge_out[part, :, cols] = d[0][tokens:].astype(half)
             out = jnp.zeros((tokens, w), jnp.float32)
             for f in each:
                 out = out + jnp.where(local[f] < 0, d[f][:tokens], 0.0)
-            gouts[i][1, part] = out.astype(half)
+            gouts[i][part] = out.astype(half)
+        when(core == 1, lambda: bwd_near1(i).start())
+        when(core == 0, lambda: bwd_near0(i).start())
+        for d, acc in ((dk, acc_k), (dv, acc_v)):
             for t in each:
                 total = jnp.where(opening[t], d[t][tokens:], 0.0)
                 if t + 1 < frames:
@@ -242,18 +252,30 @@
                 for f in range(t, frames):
                     total = total + jnp.where(local[f] == t, d[f][:tokens], 0.0)
                 acc[t, :, cols] = total
-        when(core == 1, lambda: bwd_near1(i).start())
-        when(core == 0, lambda: bwd_near0(i).start())
-        when(me > 0, lambda: bwd_edge(i).start())
+
+    def frame_outputs(i):
+        lo, w = groups[i]
+        cols = slice(lo, lo + w)
+        inside = masks(w)
+
+        def unstacked(x):
+            total = x[:tokens]
+            for h in range(1, w // head):
+                total = jnp.where(inside[h], x[h * tokens : (h + 1) * tokens], total)
+            return total.astype(half)
+
+        kcat, vcat = frame_sets(i)
+        att = [contract(pst[i][f], vcat[f], 0, 0) for f in each]
+        gq = [contract(dst[i][f], kcat[f], 0, 0) for f in each]
         for f in each:
-            att_ref[f, :, cols] = unstacked(contract(p_low[f], vcat[f], 0, 0))
-            gq_ref[f, :, cols] = unstacked(contract(ds_low[f], kcat[f], 0, 0))
+            att_ref[f, :, cols] = unstacked(att[f])
+            gq_ref[f, :, cols] = unstacked(gq[f])
 
     def chip_sum(i):
         when(core == 0, lambda: bwd_near1(i).wait_recv())
         when(core == 1, lambda: bwd_near0(i).wait_recv())
-        mine = gouts[i][1, core].astype(jnp.float32)
-        other = gins[i][1, core].astype(jnp.float32)
+        mine = gouts[i][core].astype(jnp.float32)
+        other = gins[i][core].astype(jnp.float32)
         keep_mine = jnp.logical_or(core == 0, mid_outside)
         keep_other = jnp.logical_or(core == 1, mid_outside)
         both = jnp.where(keep_mine, mine, 0.0) + jnp.where(keep_other, other, 0.0)
@@ -274,40 +296,48 @@
     def finish(i):
         lo, w = groups[i]
         cols = slice(lo, lo + w)
-        when(me + 1 < n, lambda: bwd_edge(i).wait_recv())
         bwd_tot_in(i).wait_recv()
         for part, (acc, result) in enumerate(((acc_k, gk_ref), (acc_v, gv_ref))):
             total = jnp.where(holder, gtots[i][part].astype(jnp.float32), 0.0)
-            total = total + jnp.where(mid_in_core0, gins[i][1, part].astype(jnp.float32), 0.0)
+            total = total + jnp.where(mid_in_core0, gins[i][part].astype(jnp.float32), 0.0)
             for t in range(frames):
                 value = acc[t, :, cols] + jnp.where(last_open == t, total, 0.0)
                 if t == frames - 1:
-                    behind = gins[i][0, part].astype(jnp.float32)
+                    behind = gedge_in[part, :, cols].astype(jnp.float32)
                     value = value + jnp.where(next_prev, behind, 0.0)
                 result[t, :, cols] = value.astype(half)
 
     relay(0)
     for i in range(count):
+        fwd_far_in(i).wait_recv()
+        if i == 0:
+            for part in range(2):
+                when(me > 0, lambda: fwd_edge(part).wait_recv())
+        scores(i)
         if i + 1 < count:
             relay(i + 1)
-        fwd_far_in(i).wait_recv()
-        when(me > 0, lambda: fwd_edge(i).wait_recv())
-        compute(i)
+        key_grads(i)
         if i:
             chip_sum(i - 1)
+    when(me > 0, lambda: bwd_edge().start())
+    frame_outputs(0)
     chip_sum(count - 1)
+    for i in range(1, count):
+        frame_outputs(i)
     for i in range(count):
         returned(i)
+    when(me + 1 < n, lambda: bwd_edge().wait_recv())
     for i in range(count):
         finish(i)
 
+    when(me > 0, lambda: bwd_edge().wait_send())
+    for part in range(2):
+        when(me + 1 < n, lambda: fwd_edge(part).wait_send())
     for i in range(count):
         when(core == 0, lambda: fwd_near0(i).wait_send())
         when(core == 1, lambda: fwd_near1(i).wait_send())
         when(core == 0, lambda: bwd_near0(i).wait_send())
         when(core == 1, lambda: bwd_near1(i).wait_send())
-        when(me + 1 < n, lambda: fwd_edge(i).wait_send())
-        when(me > 0, lambda: bwd_edge(i).wait_send())
         fwd_far(i).wait_send()
         bwd_tot(i).wait_send()
         for k in range(1, reach + 1):
@@ -337,17 +367,21 @@
     scratch = [pltpu.SMEM(clip_lengths.shape, jnp.int32)]
     scratch += [pltpu.VMEM((frames, tokens, width), half)] * 2
     scratch += [pltpu.VMEM((frames, tokens, width), jnp.float32)] * 2
+    scratch += [pltpu.VMEM((2, tokens, width), half)] * 3
     scratch += [pltpu.SemaphoreType.DMA((3 + 2 * count,))]
-    scratch += [pltpu.SemaphoreType.DMA((count, 3 + reach))] * 4
+    scratch += [pltpu.SemaphoreType.DMA((3,))] * 2
+    scratch += [pltpu.SemaphoreType.DMA((count, 2 + reach))] * 4
     shapes = [
         lambda w: (2, tokens, w),
-        lambda w: (frames + 3, 2, tokens, w),
+        lambda w: (frames + 2, 2, tokens, w),
         lambda w: (tokens, w),
         lambda w: (reach, tokens, w),
         lambda w: (frames, w // head * tokens, w),
         lambda w: (frames, w // head * tokens, w),
-        lambda w: (2, 2, tokens, w),
-        lambda w: (2, 2, tokens, w),
+        lambda w: (frames, 2 * tokens, w // head * tokens),
+        lambda w: (frames, 2 * tokens, w // head * tokens),
+        lambda w: (2, tokens, w),
+        lambda w: (2, tokens, w),
         lambda w: (tokens, w),
         lambda w: (reach, tokens, w),
         lambda w: (2, tokens, w),
@@ -373,7 +407,8 @@
         in_specs=[vmem] * 4,
         out_specs=[hbm] * 4,
         scratch_shapes=[pltpu.SemaphoreType.DMA((4,))],
-    )(*results)
+        compiler_params=pltpu.CompilerParams(vmem_limit_bytes=4 * 1024 * 1024),
+    )(*[pltpu.with_memory_space_constraint(a, pltpu.VMEM) for a in results])
 
 
 def solution(mesh):

time: 22.7 us -> 19.7 us (0.87)
  local copies, waits for them, and re-layouts: 2.63 us -> 0 us
  Pallas kernels: 19.2 us -> 18.8 us
    unnamed x8 -> x0, local copies, waits for them, and re-layouts: 2.63 us -> none
    pallas_call x1, Pallas kernels: 2.01 us -> 0.87 us  [body(): pl.pallas_call(store_kernel, out_shape=like, in_specs=[vmem] * 4, out_spe...]
    pallas_call x1, Pallas kernels: 17.2 us -> 17.9 us  [body(): pl.pallas_call(functools.partial(kernel, n, reach, groups, head), out_sha...]
where the time goes in v3:
time: 19.7 us; the launch traced here: 19.4 us
  Pallas kernels  18.8 us (95%)
  between operations  0.64 us (3%)
    pallas_call x1, Pallas kernels, body(): pl.pallas_call(functools.partial(kernel, n, reach, groups, head), out_sha...  17.9 us
    pallas_call x1, Pallas kernels, body(): pl.pallas_call(store_kernel, out_shape=like, in_specs=[vmem] * 4, out_spe...  0.87 us

profile of v3, /device:TPU:19, one launch (start us, length us, event | category | flops | bytes accessed | tf_op | source)
XLA Modules:
  0.0 19.4 jit_solution(8054876855837520095)
XLA Ops:
  0.6 17.9 %shard_map.84 = (bf16[4,32,640]{2,1,0:T(8,128)(2,1)S(1)}, bf16[4,32,640]{2,1,0:T(8,128)(2,1)S(1)}, bf16[4,32,640]{2,1,0:T(8,128)(2,1)S(1)}, bf16[4,32,640]{2,1,0:T(8,128)(2,1)S(1)}) custom-call(s32[16]{0:T(128)} %len_ref.1, bf16[4,32,640]{2,1,0:T(8,128)(2,1)} %q_ref.1, bf16[4,32,640]{2,1,0:T(8,128)(2,1)} %k_ref.1, bf16[4,32,640]{2,1,0:T(8,128)(2,1)} %v_ref.1, ...), custom_call_target="tpu_custom_call" | custom-call | tf_op jit(solution)/shard_map/pallas_call | solution.py:394
  18.5 0.9 %shard_map.85 = (bf16[4,32,640]{2,1,0:T(8,128)(2,1)}, bf16[4,32,640]{2,1,0:T(8,128)(2,1)}, bf16[4,32,640]{2,1,0:T(8,128)(2,1)}, bf16[4,32,640]{2,1,0:T(8,128)(2,1)}) custom-call(bf16[4,32,640]{2,1,0:T(8,128)(2,1)S(1)} %get-tuple-element.8.refs_0_, bf16[4,32,640]{2,1,0:T(8,128)(2,1)S(1)} %get-tuple-element.9.refs_1_, ...), custom_call_target="tpu_custom_call" | custom-call | tf_op jit(solution)/shard_map/pallas_call | solution.py:404

commit v4 on v3

--- a/solution.py
+++ b/solution.py
@@ -21,13 +21,12 @@
     n, reach, groups, head,
     len_ref, q_ref, k_ref, v_ref, g_ref,
     att_ref, gq_ref, gk_ref, gv_ref,
-    lens, q_all, g_all, acc_k, acc_v, edges, gedge_out, gedge_in,
-    lsem, esend, erecv, fsend, frecv, bsend, brecv, *bufs,
+    lens, q_all, g_all, acc_k, acc_v, lsem, fsend, frecv, bsend, brecv, *bufs,
 ):
     count = len(groups)
     bufs = [bufs[j * count : (j + 1) * count] for j in range(len(bufs) // count)]
     starts, pools, chip_out, chip_in, qst, gst, pst, dst = bufs[:8]
-    gouts, gins, gchip_out, gchip_in, gtots = bufs[8:]
+    gouts, gins, gchip_out, gchip_in, gtots, edges, gedge_out, gedge_in = bufs[8:]
     frames, tokens, _ = q_ref.shape
     me = lax.axis_index("tm")
     core = lax.rem(me, 2)
@@ -62,21 +61,14 @@
         @pl.when(chip + k < chips)
         def _():
             greet(me + 2 * k)
+            greet(sibling + 2 * k)
 
         @pl.when(chip >= k)
         def _():
             greet(me - 2 * k)
-
-    @pl.when(jnp.logical_and(core == 1, me + 1 < n))
-    def _():
-        greet(me + 1)
-
-    @pl.when(jnp.logical_and(core == 0, me > 0))
-    def _():
-        greet(me - 1)
-
-    greeted = 1 + jnp.minimum(reach, chips - 1 - chip) + jnp.minimum(reach, chip)
-    greeted += jnp.where(core == 1, jnp.minimum(1, n - 1 - me), jnp.minimum(1, me))
+            greet(sibling - 2 * k)
+
+    greeted = 1 + 2 * (jnp.minimum(reach, chips - 1 - chip) + jnp.minimum(reach, chip))
 
     first = me * frames
     chip_first = chip * (2 * frames)
@@ -130,9 +122,9 @@
         return ends(src, dst, send.at[i, slot], recv.at[i, slot], device)
 
     after, before = jnp.minimum(me + 1, n - 1), jnp.maximum(me - 1, 0)
-    fwd_edge = lambda part: ends(
-        (k_ref, v_ref)[part].at[frames - 1], edges.at[part], esend.at[part], erecv.at[part], after)
-    bwd_edge = lambda: ends(gedge_out, gedge_in, esend.at[2], erecv.at[2], before)
+    fwd_edge = lambda i: remote(
+        pools[i].at[frames - 1], edges[i], fsend, frecv, i, 2 + reach, after)
+    bwd_edge = lambda i: remote(gedge_out[i], gedge_in[i], bsend, brecv, i, 2 + reach, before)
     fwd_near0 = lambda i: remote(starts[i], pools[i].at[near], fsend, frecv, i, 0, sibling)
     fwd_near1 = lambda i: remote(
         starts[i].at[0], pools[i].at[near, 0], fsend, frecv, i, 0, sibling)
@@ -149,7 +141,14 @@
     bwd_tot_in = lambda i: remote(
         gtots[i].at[core], gtots[i].at[1 - core], bsend, brecv, i, 1, sibling)
     bwd_chip = lambda i, k: remote(
-        gchip_out[i], gchip_in[i].at[k - 1], bsend, brecv, i, 1 + k, jnp.maximum(me - 2 * k, 0))
+        gchip_out[i], gchip_in[i].at[core, k - 1], bsend, brecv, i, 1 + k,
+        jnp.maximum(me - 2 * k, 0))
+    bwd_cross = lambda i, k: remote(
+        gchip_out[i], gchip_in[i].at[core, k - 1], bsend, brecv, i, 2 + reach + k,
+        jnp.maximum(sibling - 2 * k, 0))
+    bwd_cross_in = lambda i, k: remote(
+        gchip_out[i], gchip_in[i].at[1 - core, k - 1], bsend, brecv, i, 2 + reach + k,
+        jnp.maximum(sibling - 2 * k, 0))
 
     def when(condition, act):
         @pl.when(condition)
@@ -168,8 +167,7 @@
     for i in range(count):
         when(core == 0, lambda: fwd_near0(i).start())
         when(core == 1, lambda: fwd_near1(i).start())
-    for part in range(2):
-        when(me + 1 < n, lambda: fwd_edge(part).start())
+    when(me + 1 < n, lambda: fwd_edge(0).start())
 
     for i in range(count):
         when(core == 1, lambda: fwd_near0(i).wait_recv())
@@ -179,6 +177,8 @@
         chip_out[i][...] = jnp.where(take_own, own, other)
         for k in range(1, reach + 1):
             when(chip + k < chips, lambda: fwd_chip(i, k).start())
+        if i + 1 < count:
+            when(me + 1 < n, lambda: fwd_edge(i + 1).start())
 
     for copy in late:
         copy.wait()
@@ -211,9 +211,8 @@
     each = range(frames)
 
     def frame_sets(i):
-        lo, w = groups[i]
         own = [pools[i][owner_slot[f]] for f in each]
-        prev = [jnp.where(opening[0], pools[i][0], edges[:, :, lo : lo + w])]
+        prev = [jnp.where(opening[0], pools[i][0], edges[i][...])]
         prev += [pools[i][prev_slot[f - 1]] for f in each[1:]]
         return [
             [jnp.concatenate([own[f][part], prev[f][part]], axis=0) for f in each]
@@ -224,6 +223,8 @@
         kcat, vcat = frame_sets(i)
         s = [contract(kcat[f], qst[i][f], 1, 1) * scale for f in each]
         dp = [contract(vcat[f], gst[i][f], 1, 1) for f in each]
+        if i:
+            frame_outputs(i - 1)
         e = [jnp.exp(s[f] - jnp.max(s[f], axis=0, keepdims=True)) for f in each]
         p = [e[f] * (1.0 / jnp.sum(e[f], axis=0, keepdims=True)) for f in each]
         ds = [p[f] * (dp[f] - jnp.sum(p[f] * dp[f], axis=0, keepdims=True)) * scale for f in each]
@@ -237,13 +238,14 @@
         dk = [contract(dst[i][f], qst[i][f], 1, 0) for f in each]
         dv = [contract(pst[i][f], gst[i][f], 1, 0) for f in each]
         for part, d in enumerate((dk, dv)):
-            gedge_out[part, :, cols] = d[0][tokens:].astype(half)
+            gedge_out[i][part] = d[0][tokens:].astype(half)
             out = jnp.zeros((tokens, w), jnp.float32)
             for f in each:
                 out = out + jnp.where(local[f] < 0, d[f][:tokens], 0.0)
             gouts[i][part] = out.astype(half)
         when(core == 1, lambda: bwd_near1(i).start())
         when(core == 0, lambda: bwd_near0(i).start())
+        when(me > 0, lambda: bwd_edge(i).start())
         for d, acc in ((dk, acc_k), (dv, acc_v)):
             for t in each:
                 total = jnp.where(opening[t], d[t][tokens:], 0.0)
@@ -282,67 +284,73 @@
         gchip_out[i][...] = both.astype(half)
         for k in range(1, reach + 1):
             when(chip >= k, lambda: bwd_chip(i, k).start())
+            if i == count - 1:
+                when(chip >= k, lambda: bwd_cross(i, k).start())
 
     def returned(i):
+        both = i == count - 1
         for k in range(1, reach + 1):
             when(chip + k < chips, lambda: bwd_chip(i, k).wait_recv())
-        total = None
-        for k in range(1, reach + 1):
-            term = jnp.where(returns[k - 1], gchip_in[i][k - 1].astype(jnp.float32), 0.0)
-            total = term if total is None else total + term
-        gtots[i][core] = total.astype(half)
-        bwd_tot(i).start()
+            if both:
+                when(chip + k < chips, lambda: bwd_cross_in(i, k).wait_recv())
+        for part in (0, 1) if both else (core,):
+            total = None
+            for k in range(1, reach + 1):
+                term = gchip_in[i][part, k - 1].astype(jnp.float32)
+                term = jnp.where(returns[k - 1], term, 0.0)
+                total = term if total is None else total + term
+            gtots[i][part] = total.astype(half)
+        if not both:
+            bwd_tot(i).start()
 
     def finish(i):
         lo, w = groups[i]
         cols = slice(lo, lo + w)
-        bwd_tot_in(i).wait_recv()
+        when(me + 1 < n, lambda: bwd_edge(i).wait_recv())
+        if i < count - 1:
+            bwd_tot_in(i).wait_recv()
         for part, (acc, result) in enumerate(((acc_k, gk_ref), (acc_v, gv_ref))):
             total = jnp.where(holder, gtots[i][part].astype(jnp.float32), 0.0)
             total = total + jnp.where(mid_in_core0, gins[i][part].astype(jnp.float32), 0.0)
             for t in range(frames):
                 value = acc[t, :, cols] + jnp.where(last_open == t, total, 0.0)
                 if t == frames - 1:
-                    behind = gedge_in[part, :, cols].astype(jnp.float32)
+                    behind = gedge_in[i][part].astype(jnp.float32)
                     value = value + jnp.where(next_prev, behind, 0.0)
                 result[t, :, cols] = value.astype(half)
 
     relay(0)
     for i in range(count):
         fwd_far_in(i).wait_recv()
-        if i == 0:
-            for part in range(2):
-                when(me > 0, lambda: fwd_edge(part).wait_recv())
+        when(me > 0, lambda: fwd_edge(i).wait_recv())
         scores(i)
         if i + 1 < count:
             relay(i + 1)
         key_grads(i)
         if i:
             chip_sum(i - 1)
-    when(me > 0, lambda: bwd_edge().start())
-    frame_outputs(0)
     chip_sum(count - 1)
-    for i in range(1, count):
-        frame_outputs(i)
+    frame_outputs(count - 1)
     for i in range(count):
         returned(i)
-    when(me + 1 < n, lambda: bwd_edge().wait_recv())
     for i in range(count):
         finish(i)
 
-    when(me > 0, lambda: bwd_edge().wait_send())
-    for part in range(2):
-        when(me + 1 < n, lambda: fwd_edge(part).wait_send())
     for i in range(count):
         when(core == 0, lambda: fwd_near0(i).wait_send())
         when(core == 1, lambda: fwd_near1(i).wait_send())
         when(core == 0, lambda: bwd_near0(i).wait_send())
         when(core == 1, lambda: bwd_near1(i).wait_send())
+        when(me + 1 < n, lambda: fwd_edge(i).wait_send())
+        when(me > 0, lambda: bwd_edge(i).wait_send())
         fwd_far(i).wait_send()
-        bwd_tot(i).wait_send()
+        if i < count - 1:
+            bwd_tot(i).wait_send()
         for k in range(1, reach + 1):
             when(chip + k < chips, lambda: fwd_chip(i, k).wait_send())
             when(chip >= k, lambda: bwd_chip(i, k).wait_send())
+            if i == count - 1:
+                when(chip >= k, lambda: bwd_cross(i, k).wait_send())
 
 
 def store_kernel(*refs):
@@ -367,10 +375,8 @@
     scratch = [pltpu.SMEM(clip_lengths.shape, jnp.int32)]
     scratch += [pltpu.VMEM((frames, tokens, width), half)] * 2
     scratch += [pltpu.VMEM((frames, tokens, width), jnp.float32)] * 2
-    scratch += [pltpu.VMEM((2, tokens, width), half)] * 3
     scratch += [pltpu.SemaphoreType.DMA((3 + 2 * count,))]
-    scratch += [pltpu.SemaphoreType.DMA((3,))] * 2
-    scratch += [pltpu.SemaphoreType.DMA((count, 2 + reach))] * 4
+    scratch += [pltpu.SemaphoreType.DMA((count, 3 + 2 * reach))] * 4
     shapes = [
         lambda w: (2, tokens, w),
         lambda w: (frames + 2, 2, tokens, w),
@@ -383,7 +389,10 @@
         lambda w: (2, tokens, w),
         lambda w: (2, tokens, w),
         lambda w: (tokens, w),
-        lambda w: (reach, tokens, w),
+        lambda w: (2, reach, tokens, w),
+        lambda w: (2, tokens, w),
+        lambda w: (2, tokens, w),
+        lambda w: (2, tokens, w),
         lambda w: (2, tokens, w),
     ]
     scratch += [pltpu.VMEM(shape(w), half) for shape in shapes for _, w in groups]

time: 19.7 us -> 19.8 us (level)
  the two profiles are of different devices: /device:TPU:19 before, /device:TPU:0 now
where the time goes in v4:
time: 19.8 us; the launch traced here: 19.6 us
  Pallas kernels  19 us (96%)
  between operations  0.64 us (3%)
    pallas_call x1, Pallas kernels, body(): pl.pallas_call(functools.partial(kernel, n, reach, groups, head), out_sha...  18.1 us
    pallas_call x1, Pallas kernels, body(): pl.pallas_call(store_kernel, out_shape=like, in_specs=[vmem] * 4, out_spe...  0.87 us

profile of v4, /device:TPU:0, one launch (start us, length us, event | category | flops | bytes accessed | tf_op | source)
XLA Modules:
  0.0 19.6 jit_solution(12326527080700558501)
XLA Ops:
  0.6 18.1 %shard_map.84 = (bf16[4,32,640]{2,1,0:T(8,128)(2,1)S(1)}, bf16[4,32,640]{2,1,0:T(8,128)(2,1)S(1)}, bf16[4,32,640]{2,1,0:T(8,128)(2,1)S(1)}, bf16[4,32,640]{2,1,0:T(8,128)(2,1)S(1)}) custom-call(s32[16]{0:T(128)} %len_ref.1, bf16[4,32,640]{2,1,0:T(8,128)(2,1)} %q_ref.1, bf16[4,32,640]{2,1,0:T(8,128)(2,1)} %k_ref.1, bf16[4,32,640]{2,1,0:T(8,128)(2,1)} %v_ref.1, ...), custom_call_target="tpu_custom_call" | custom-call | tf_op jit(solution)/shard_map/pallas_call | solution.py:403
  18.7 0.9 %shard_map.85 = (bf16[4,32,640]{2,1,0:T(8,128)(2,1)}, bf16[4,32,640]{2,1,0:T(8,128)(2,1)}, bf16[4,32,640]{2,1,0:T(8,128)(2,1)}, bf16[4,32,640]{2,1,0:T(8,128)(2,1)}) custom-call(bf16[4,32,640]{2,1,0:T(8,128)(2,1)S(1)} %get-tuple-element.8.refs_0_, bf16[4,32,640]{2,1,0:T(8,128)(2,1)S(1)} %get-tuple-element.9.refs_1_, ...), custom_call_target="tpu_custom_call" | custom-call | tf_op jit(solution)/shard_map/pallas_call | solution.py:413

commit v5 on v3

v5 whole, which is shorter than its diff:
```python
import functools

import jax
import jax.numpy as jnp
from jax import lax
from jax.experimental import pallas as pl
from jax.experimental.pallas import tpu as pltpu
from jax.sharding import PartitionSpec as P

HEADS = 10
MAXCLIP = 24
MESH = pl.DeviceIdType.MESH


def lane_groups(width, head):
    step = max(256, head)
    tiles = [(start, min(step, width - start)) for start in range(0, width, step)]
    groups = []
    for part in (list(enumerate(tiles))[:1], list(enumerate(tiles))[1:]):
        if part:
            lo = part[0][1][0]
            subs = [(j, start - lo, w) for j, (start, w) in part]
            groups.append((lo, sum(w for _, _, w in subs), subs))
    return tiles, groups


def kernel(
    n, reach, tiles, groups, head,
    len_ref, q_ref, k_ref, v_ref, g_ref,
    att_ref, gq_ref, gk_ref, gv_ref,
    lens, q_all, g_all, acc_k, acc_v, lsem, fsend, frecv, bsend, brecv, *bufs,
):
    count = len(groups)
    qst, gst, pst, dst = [bufs[j * len(tiles) : (j + 1) * len(tiles)] for j in range(4)]
    bufs = bufs[4 * len(tiles) :]
    bufs = [bufs[j * count : (j + 1) * count] for j in range(len(bufs) // count)]
    starts, pools, chip_out, chip_in = bufs[:4]
    gouts, gins, gchip_out, gchip_in, gtots, edges, gedge_out, gedge_in = bufs[4:]
    frames, tokens, _ = q_ref.shape
    me = lax.axis_index("tm")
    core = lax.rem(me, 2)
    chip = lax.div(me, 2)
    chips = n // 2
    sibling = me + 1 - 2 * core
    scale = head ** (-0.5)
    near, far = frames, frames + 1
    half = jnp.bfloat16

    loads = [pltpu.make_async_copy(len_ref, lens, lsem.at[0])]
    for i, (lo, w, _) in enumerate(groups):
        for part, ref in enumerate((k_ref, v_ref)):
            loads.append(pltpu.make_async_copy(
                ref.at[:, :, pl.ds(lo, w)], pools[i].at[pl.ds(0, frames), part],
                lsem.at[1 + 2 * i + part],
            ))
    late = [
        pltpu.make_async_copy(q_ref, q_all, lsem.at[1 + 2 * count]),
        pltpu.make_async_copy(g_ref, g_all, lsem.at[2 + 2 * count]),
    ]
    for copy in loads + late:
        copy.start()

    barrier = pltpu.get_barrier_semaphore()

    def greet(device):
        pl.semaphore_signal(barrier, inc=1, device_id=(device,), device_id_type=MESH)

    def ahead(steps):
        return lax.rem(me + steps + n, n)

    greet(ahead(1))
    greet(ahead(-1))
    for k in range(1, reach + 1):
        greet(ahead(2 * k))
        greet(ahead(-2 * k))
    greeted = 2 + 2 * reach

    first = me * frames
    chip_first = chip * (2 * frames)
    wanted = [first + f for f in range(frames)]
    wanted += [chip_first, chip_first + frames, chip_first + 2 * frames - 1]
    wanted += [chip_first + k * 2 * frames for k in range(1, reach + 1)]
    loads[0].wait()

    def scan_clips(c, carry):
        start, owners = carry
        owners = tuple(jnp.where(start <= w, start, o) for w, o in zip(wanted, owners))
        return start + lens[c], owners

    zero = jnp.int32(0)
    _, owners = lax.fori_loop(0, len_ref.shape[0], scan_clips, (zero, (zero,) * len(wanted)))
    own_first, own_mid, own_last = owners[frames : frames + 3]
    own_later = owners[frames + 3 :]
    local = [owners[f] - first for f in range(frames)]
    opening = [local[f] == f for f in range(frames)]
    last_open = jnp.clip(local[frames - 1], 0, frames - 1)
    back = jnp.clip(chip - lax.div(own_first, jnp.int32(2 * frames)), 1, reach)
    away = [
        jnp.where(jnp.logical_and(core == 1, owners[f] >= chip_first), near, far)
        for f in range(frames)
    ]
    owner_slot = [jnp.where(local[f] >= 0, local[f], away[f]) for f in range(frames)]
    prev_slot = [jnp.where(opening[f], f, f - 1) for f in range(1, frames)]
    last_in_core1 = own_last >= chip_first + frames
    mid_outside = own_mid < chip_first
    mid_in_core0 = jnp.logical_and(
        core == 0, jnp.logical_and(own_mid >= chip_first, own_mid < chip_first + frames)
    )
    returns = [
        jnp.logical_and(
            chip + k < chips,
            jnp.logical_and(own_later[k - 1] >= chip_first, own_later[k - 1] < chip_first + 2 * frames),
        )
        for k in range(1, reach + 1)
    ]
    holder = jnp.logical_and(own_last >= first, own_last < first + frames)
    next_first = jnp.where(core == 0, own_mid, own_later[0])
    next_prev = jnp.logical_and(next_first != first + frames, me + 1 < n)

    def ends(src, dst, send_sem, recv_sem, device):
        return pltpu.make_async_remote_copy(
            src_ref=src, dst_ref=dst, send_sem=send_sem, recv_sem=recv_sem,
            device_id=(device,), device_id_type=MESH,
        )

    def remote(src, dst, send, recv, i, slot, device):
        return ends(src, dst, send.at[i, slot], recv.at[i, slot], device)

    fwd_edge = lambda i: remote(
        pools[i].at[frames - 1], edges[i], fsend, frecv, i, 3, ahead(1))
    fwd_near = lambda i: remote(starts[i], pools[i].at[near], fsend, frecv, i, 0, sibling)
    fwd_far = lambda i: remote(
        pools[i].at[far, core], pools[i].at[far, core], fsend, frecv, i, 1, sibling)
    fwd_far_in = lambda i: remote(
        pools[i].at[far, core], pools[i].at[far, 1 - core], fsend, frecv, i, 1, sibling)
    fwd_chip = lambda i, k: remote(
        chip_out[i], chip_in[i].at[k - 1], fsend, frecv, i, 2, ahead(2 * k))
    fwd_chips = lambda i: remote(chip_in[i], chip_in[i], fsend, frecv, i, 2, sibling)
    bwd_edge = lambda i: remote(gedge_out[i], gedge_in[i], bsend, brecv, i, 3, ahead(-1))
    bwd_near = lambda i: remote(gouts[i], gins[i], bsend, brecv, i, 0, sibling)
    bwd_tot = lambda i: remote(
        gtots[i].at[core], gtots[i].at[core], bsend, brecv, i, 1, sibling)
    bwd_tot_in = lambda i: remote(
        gtots[i].at[core], gtots[i].at[1 - core], bsend, brecv, i, 1, sibling)
    bwd_chip = lambda i, k: remote(
        gchip_out[i], gchip_in[i].at[k - 1], bsend, brecv, i, 2, ahead(-2 * k))
    bwd_chips = lambda i: remote(gchip_in[i], gchip_in[i], bsend, brecv, i, 2, sibling)

    for copy in loads[1:]:
        copy.wait()
    for i in range(count):
        start = pools[i][0]
        for f in range(1, frames):
            start = jnp.where(last_open == f, pools[i][f], start)
        starts[i][...] = start
    pl.semaphore_wait(barrier, greeted)

    for i in range(count):
        fwd_near(i).start()
    fwd_edge(0).start()

    for i in range(count):
        fwd_near(i).wait_recv()
        own, other = starts[i][core], pools[i][near, core]
        take_own = jnp.where(core == 1, last_in_core1, jnp.logical_not(last_in_core1))
        chip_out[i][...] = jnp.where(take_own, own, other)
        for k in range(1, reach + 1):
            fwd_chip(i, k).start()
        if i + 1 < count:
            fwd_edge(i + 1).start()

    for copy in late:
        copy.wait()

    def masks(w):
        lane = lax.broadcasted_iota(jnp.int32, (tokens, w), 1)
        return [
            jnp.logical_and(lane >= h * head, lane < (h + 1) * head) for h in range(w // head)
        ]

    for j, (lo, w) in enumerate(tiles):
        keep = [m.astype(jnp.float32).astype(half) for m in masks(w)]
        for f in range(frames):
            for h, m in enumerate(keep):
                rows = slice(h * tokens, (h + 1) * tokens)
                qst[j][f, rows] = q_all[f, :, lo : lo + w] * m
                gst[j][f, rows] = g_all[f, :, lo : lo + w] * m

    def contract(a, b, ca, cb):
        return lax.dot_general(
            a, b, (((ca,), (cb,)), ((), ())), preferred_element_type=jnp.float32
        )

    def relay(i):
        fwd_chips(i).wait_recv()
        pools[i][far, core] = chip_in[i][back - 1]
        fwd_far(i).start()

    each = range(frames)

    def frame_sets(i):
        own = [pools[i][owner_slot[f]] for f in each]
        prev = [jnp.where(opening[0], pools[i][0], edges[i][...])]
        prev += [pools[i][prev_slot[f - 1]] for f in each[1:]]
        return [
            [jnp.concatenate([own[f][part], prev[f][part]], axis=0) for f in each]
            for part in range(2)
        ]

    def scores(i):
        kcat, vcat = frame_sets(i)
        pairs = [(f, j, slice(off, off + w)) for j, off, w in groups[i][2] for f in each]
        s = [contract(kcat[f][:, c], qst[j][f], 1, 1) * scale for f, j, c in pairs]
        dp = [contract(vcat[f][:, c], gst[j][f], 1, 1) for f, j, c in pairs]
        if i:
            frame_outputs(i - 1)
        e = [jnp.exp(x - jnp.max(x, axis=0, keepdims=True)) for x in s]
        p = [x * (1.0 / jnp.sum(x, axis=0, keepdims=True)) for x in e]
        for (f, j, _), x, d in zip(pairs, p, dp):
            pst[j][f] = x.astype(half)
            dst[j][f] = (x * (d - jnp.sum(x * d, axis=0, keepdims=True)) * scale).astype(half)

    def key_grads(i):
        lo = groups[i][0]
        for j, off, w in groups[i][2]:
            here, cols = slice(off, off + w), slice(lo + off, lo + off + w)
            dk = [contract(dst[j][f], qst[j][f], 1, 0) for f in each]
            dv = [contract(pst[j][f], gst[j][f], 1, 0) for f in each]
            for part, (d, acc) in enumerate(((dk, acc_k), (dv, acc_v))):
                gedge_out[i][part, :, here] = d[0][tokens:].astype(half)
                out = jnp.zeros((tokens, w), jnp.float32)
                for f in each:
                    out = out + jnp.where(local[f] < 0, d[f][:tokens], 0.0)
                gouts[i][part, :, here] = out.astype(half)
                for t in each:
                    total = jnp.where(opening[t], d[t][tokens:], 0.0)
                    if t + 1 < frames:
                        total = total + jnp.where(opening[t + 1], 0.0, d[t + 1][tokens:])
                    for f in range(t, frames):
                        total = total + jnp.where(local[f] == t, d[f][:tokens], 0.0)
                    acc[t, :, cols] = total
        bwd_near(i).start()
        bwd_edge(i).start()

    def frame_outputs(i):
        lo = groups[i][0]
        kcat, vcat = frame_sets(i)
        for j, off, w in groups[i][2]:
            here, cols = slice(off, off + w), slice(lo + off, lo + off + w)
            inside = masks(w)

            def unstacked(x):
                total = x[:tokens]
                for h in range(1, w // head):
                    total = jnp.where(inside[h], x[h * tokens : (h + 1) * tokens], total)
                return total.astype(half)

            att = [contract(pst[j][f], vcat[f][:, here], 0, 0) for f in each]
            gq = [contract(dst[j][f], kcat[f][:, here], 0, 0) for f in each]
            for f in each:
                att_ref[f, :, cols] = unstacked(att[f])
                gq_ref[f, :, cols] = unstacked(gq[f])

    def chip_sum(i):
        bwd_near(i).wait_recv()
        mine = gouts[i][core].astype(jnp.float32)
        other = gins[i][core].astype(jnp.float32)
        keep_mine = jnp.logical_or(core == 0, mid_outside)
        keep_other = jnp.logical_or(core == 1, mid_outside)
        both = jnp.where(keep_mine, mine, 0.0) + jnp.where(keep_other, other, 0.0)
        gchip_out[i][...] = both.astype(half)
        for k in range(1, reach + 1):
            bwd_chip(i, k).start()

    def returned(i):
        bwd_chips(i).wait_recv()
        total = None
        for k in range(1, reach + 1):
            term = jnp.where(returns[k - 1], gchip_in[i][k - 1].astype(jnp.float32), 0.0)
            total = term if total is None else total + term
        gtots[i][core] = total.astype(half)
        bwd_tot(i).start()

    def finish(i):
        lo, w, _ = groups[i]
        cols = slice(lo, lo + w)
        bwd_edge(i).wait_recv()
        bwd_tot_in(i).wait_recv()
        for part, (acc, result) in enumerate(((acc_k, gk_ref), (acc_v, gv_ref))):
            total = jnp.where(holder, gtots[i][part].astype(jnp.float32), 0.0)
            total = total + jnp.where(mid_in_core0, gins[i][part].astype(jnp.float32), 0.0)
            for t in range(frames):
                value = acc[t, :, cols] + jnp.where(last_open == t, total, 0.0)
                if t == frames - 1:
                    behind = gedge_in[i][part].astype(jnp.float32)
                    value = value + jnp.where(next_prev, behind, 0.0)
                result[t, :, cols] = value.astype(half)

    relay(0)
    for i in range(count):
        fwd_far_in(i).wait_recv()
        fwd_edge(i).wait_recv()
        scores(i)
        if i + 1 < count:
            relay(i + 1)
        key_grads(i)
        if i:
            chip_sum(i - 1)
    chip_sum(count - 1)
    frame_outputs(count - 1)
    for i in range(count):
        returned(i)
    for i in range(count):
        finish(i)

    for i in range(count):
        for copy in (fwd_near, fwd_edge, fwd_far, fwd_chips, bwd_near, bwd_edge, bwd_tot, bwd_chips):
            copy(i).wait_send()


def store_kernel(*refs):
    count = len(refs) // 2
    sems = refs[-1]
    copies = [
        pltpu.make_async_copy(refs[j], refs[count + j], sems.at[j]) for j in range(count)
    ]
    for copy in copies:
        copy.start()
    for copy in copies:
        copy.wait()


def body(n, queries, keys, values, out_grad, clip_lengths):
    frames, tokens, width = queries.shape
    head = width // HEADS
    reach = min(n // 2 - 1, -(-(MAXCLIP - 1) // (2 * frames)))
    tiles, groups = lane_groups(width, head)
    count = len(groups)
    half = jnp.bfloat16
    scratch = [pltpu.SMEM(clip_lengths.shape, jnp.int32)]
    scratch += [pltpu.VMEM((frames, tokens, width), half)] * 2
    scratch += [pltpu.VMEM((frames, tokens, width), jnp.float32)] * 2
    scratch += [pltpu.SemaphoreType.DMA((3 + 2 * count,))]
    scratch += [pltpu.SemaphoreType.DMA((count, 4))] * 4
    stacked = [pltpu.VMEM((frames, w // head * tokens, w), half) for _, w in tiles]
    probs = [pltpu.VMEM((frames, 2 * tokens, w // head * tokens), half) for _, w in tiles]
    scratch += stacked * 2 + probs * 2
    shapes = [
        lambda w: (2, tokens, w),
        lambda w: (frames + 2, 2, tokens, w),
        lambda w: (tokens, w),
        lambda w: (reach, tokens, w),
        lambda w: (2, tokens, w),
        lambda w: (2, tokens, w),
        lambda w: (tokens, w),
        lambda w: (reach, tokens, w),
        lambda w: (2, tokens, w),
        lambda w: (2, tokens, w),
        lambda w: (2, tokens, w),
        lambda w: (2, tokens, w),
    ]
    scratch += [pltpu.VMEM(shape(w), half) for shape in shapes for _, w, _ in groups]
    vmem = pl.BlockSpec(memory_space=pltpu.VMEM)
    hbm = pl.BlockSpec(memory_space=pltpu.HBM)
    like = [jax.ShapeDtypeStruct(queries.shape, half)] * 4
    args = (clip_lengths, queries, keys, values, out_grad)
    results = pl.pallas_call(
        functools.partial(kernel, n, reach, tiles, groups, head),
        out_shape=like,
        in_specs=[hbm] * 5,
        out_specs=[vmem] * 4,
        scratch_shapes=scratch,
        compiler_params=pltpu.CompilerParams(
            collective_id=0, has_side_effects=True, vmem_limit_bytes=48 * 1024 * 1024
        ),
    )(*[pltpu.with_memory_space_constraint(a, pltpu.HBM) for a in args])
    return pl.pallas_call(
        store_kernel,
        out_shape=like,
        in_specs=[vmem] * 4,
        out_specs=[hbm] * 4,
        scratch_shapes=[pltpu.SemaphoreType.DMA((4,))],
        compiler_params=pltpu.CompilerParams(vmem_limit_bytes=4 * 1024 * 1024),
    )(*[pltpu.with_memory_space_constraint(a, pltpu.VMEM) for a in results])


def solution(mesh):
    split = P("tm", None, None)
    return jax.shard_map(
        functools.partial(body, mesh.shape["tm"]),
        mesh=mesh,
        in_specs=(split,) * 4 + (P(),),
        out_specs=(split,) * 4,
        check_vma=False,
    )
```

time: 19.7 us -> 21.5 us (1.091)
  the two profiles are of different devices: /device:TPU:19 before, /device:TPU:0 now
where the time goes in v5:
time: 21.5 us; the launch traced here: 21.4 us
  Pallas kernels  20.7 us (96%)
  between operations  0.64 us (3%)
    pallas_call x1, Pallas kernels, body(): pl.pallas_call(functools.partial(kernel, n, reach, tiles, groups, head),...  19.9 us
    pallas_call x1, Pallas kernels, body(): pl.pallas_call(store_kernel, out_shape=like, in_specs=[vmem] * 4, out_spe...  0.87 us

profile of v5, /device:TPU:0, one launch (start us, length us, event | category | flops | bytes accessed | tf_op | source)
XLA Modules:
  0.0 21.4 jit_solution(9286960243394678608)
XLA Ops:
  0.6 19.9 %shard_map.84 = (bf16[4,32,640]{2,1,0:T(8,128)(2,1)S(1)}, bf16[4,32,640]{2,1,0:T(8,128)(2,1)S(1)}, bf16[4,32,640]{2,1,0:T(8,128)(2,1)S(1)}, bf16[4,32,640]{2,1,0:T(8,128)(2,1)S(1)}) custom-call(s32[16]{0:T(128)} %len_ref.1, bf16[4,32,640]{2,1,0:T(8,128)(2,1)} %q_ref.1, bf16[4,32,640]{2,1,0:T(8,128)(2,1)} %k_ref.1, bf16[4,32,640]{2,1,0:T(8,128)(2,1)} %v_ref.1, ...), custom_call_target="tpu_custom_call" | custom-call | tf_op jit(solution)/shard_map/pallas_call | solution.py:367
  20.5 0.9 %shard_map.85 = (bf16[4,32,640]{2,1,0:T(8,128)(2,1)}, bf16[4,32,640]{2,1,0:T(8,128)(2,1)}, bf16[4,32,640]{2,1,0:T(8,128)(2,1)}, bf16[4,32,640]{2,1,0:T(8,128)(2,1)}) custom-call(bf16[4,32,640]{2,1,0:T(8,128)(2,1)S(1)} %get-tuple-element.8.refs_0_, bf16[4,32,640]{2,1,0:T(8,128)(2,1)S(1)} %get-tuple-element.9.refs_1_, ...), custom_call_target="tpu_custom_call" | custom-call | tf_op jit(solution)/shard_map/pallas_call | solution.py:377

commit v6 on v5

--- a/solution.py
+++ b/solution.py
@@ -68,12 +68,18 @@
     def ahead(steps):
         return lax.rem(me + steps + n, n)
 
-    greet(ahead(1))
-    greet(ahead(-1))
+    def when(condition, act):
+        @pl.when(condition)
+        def _():
+            act()
+
+    when(me + 1 < n, lambda: greet(ahead(1)))
+    when(me > 0, lambda: greet(ahead(-1)))
     for k in range(1, reach + 1):
-        greet(ahead(2 * k))
-        greet(ahead(-2 * k))
-    greeted = 2 + 2 * reach
+        when(chip + k < chips, lambda: greet(ahead(2 * k)))
+        when(chip >= k, lambda: greet(ahead(-2 * k)))
+    greeted = jnp.minimum(1, me) + jnp.minimum(1, n - 1 - me)
+    greeted += jnp.minimum(reach, chips - 1 - chip) + jnp.minimum(reach, chip)
 
     first = me * frames
     chip_first = chip * (2 * frames)
@@ -127,24 +133,22 @@
         return ends(src, dst, send.at[i, slot], recv.at[i, slot], device)
 
     fwd_edge = lambda i: remote(
-        pools[i].at[frames - 1], edges[i], fsend, frecv, i, 3, ahead(1))
+        pools[i].at[frames - 1], edges[i], fsend, frecv, i, 2, ahead(1))
     fwd_near = lambda i: remote(starts[i], pools[i].at[near], fsend, frecv, i, 0, sibling)
     fwd_far = lambda i: remote(
         pools[i].at[far, core], pools[i].at[far, core], fsend, frecv, i, 1, sibling)
     fwd_far_in = lambda i: remote(
         pools[i].at[far, core], pools[i].at[far, 1 - core], fsend, frecv, i, 1, sibling)
     fwd_chip = lambda i, k: remote(
-        chip_out[i], chip_in[i].at[k - 1], fsend, frecv, i, 2, ahead(2 * k))
-    fwd_chips = lambda i: remote(chip_in[i], chip_in[i], fsend, frecv, i, 2, sibling)
-    bwd_edge = lambda i: remote(gedge_out[i], gedge_in[i], bsend, brecv, i, 3, ahead(-1))
+        chip_out[i], chip_in[i].at[k - 1], fsend, frecv, i, 3 + k, ahead(2 * k))
+    bwd_edge = lambda i: remote(gedge_out[i], gedge_in[i], bsend, brecv, i, 2, ahead(-1))
     bwd_near = lambda i: remote(gouts[i], gins[i], bsend, brecv, i, 0, sibling)
     bwd_tot = lambda i: remote(
         gtots[i].at[core], gtots[i].at[core], bsend, brecv, i, 1, sibling)
     bwd_tot_in = lambda i: remote(
         gtots[i].at[core], gtots[i].at[1 - core], bsend, brecv, i, 1, sibling)
     bwd_chip = lambda i, k: remote(
-        gchip_out[i], gchip_in[i].at[k - 1], bsend, brecv, i, 2, ahead(-2 * k))
-    bwd_chips = lambda i: remote(gchip_in[i], gchip_in[i], bsend, brecv, i, 2, sibling)
+        gchip_out[i], gchip_in[i].at[k - 1], bsend, brecv, i, 3 + k, ahead(-2 * k))
 
     for copy in loads[1:]:
         copy.wait()
@@ -157,7 +161,7 @@
 
     for i in range(count):
         fwd_near(i).start()
-    fwd_edge(0).start()
+    when(me + 1 < n, lambda: fwd_edge(0).start())
 
     for i in range(count):
         fwd_near(i).wait_recv()
@@ -165,9 +169,9 @@
         take_own = jnp.where(core == 1, last_in_core1, jnp.logical_not(last_in_core1))
         chip_out[i][...] = jnp.where(take_own, own, other)
         for k in range(1, reach + 1):
-            fwd_chip(i, k).start()
+            when(chip + k < chips, lambda: fwd_chip(i, k).start())
         if i + 1 < count:
-            fwd_edge(i + 1).start()
+            when(me + 1 < n, lambda: fwd_edge(i + 1).start())
 
     for copy in late:
         copy.wait()
@@ -192,7 +196,8 @@
         )
 
     def relay(i):
-        fwd_chips(i).wait_recv()
+        for k in range(1, reach + 1):
+            when(chip >= k, lambda: fwd_chip(i, k).wait_recv())
         pools[i][far, core] = chip_in[i][back - 1]
         fwd_far(i).start()
 
@@ -240,7 +245,7 @@
                         total = total + jnp.where(local[f] == t, d[f][:tokens], 0.0)
                     acc[t, :, cols] = total
         bwd_near(i).start()
-        bwd_edge(i).start()
+        when(me > 0, lambda: bwd_edge(i).start())
 
     def frame_outputs(i):
         lo = groups[i][0]
@@ -270,10 +275,11 @@
         both = jnp.where(keep_mine, mine, 0.0) + jnp.where(keep_other, other, 0.0)
         gchip_out[i][...] = both.astype(half)
         for k in range(1, reach + 1):
-            bwd_chip(i, k).start()
+            when(chip >= k, lambda: bwd_chip(i, k).start())
 
     def returned(i):
-        bwd_chips(i).wait_recv()
+        for k in range(1, reach + 1):
+            when(chip + k < chips, lambda: bwd_chip(i, k).wait_recv())
         total = None
         for k in range(1, reach + 1):
             term = jnp.where(returns[k - 1], gchip_in[i][k - 1].astype(jnp.float32), 0.0)
@@ -284,7 +290,7 @@
     def finish(i):
         lo, w, _ = groups[i]
         cols = slice(lo, lo + w)
-        bwd_edge(i).wait_recv()
+        when(me + 1 < n, lambda: bwd_edge(i).wait_recv())
         bwd_tot_in(i).wait_recv()
         for part, (acc, result) in enumerate(((acc_k, gk_ref), (acc_v, gv_ref))):
             total = jnp.where(holder, gtots[i][part].astype(jnp.float32), 0.0)
@@ -299,7 +305,7 @@
     relay(0)
     for i in range(count):
         fwd_far_in(i).wait_recv()
-        fwd_edge(i).wait_recv()
+        when(me > 0, lambda: fwd_edge(i).wait_recv())
         scores(i)
         if i + 1 < count:
             relay(i + 1)
@@ -314,8 +320,13 @@
         finish(i)
 
     for i in range(count):
-        for copy in (fwd_near, fwd_edge, fwd_far, fwd_chips, bwd_near, bwd_edge, bwd_tot, bwd_chips):
+        for copy in (fwd_near, fwd_far, bwd_near, bwd_tot):
             copy(i).wait_send()
+        when(me + 1 < n, lambda: fwd_edge(i).wait_send())
+        when(me > 0, lambda: bwd_edge(i).wait_send())
+        for k in range(1, reach + 1):
+            when(chip + k < chips, lambda: fwd_chip(i, k).wait_send())
+            when(chip >= k, lambda: bwd_chip(i, k).wait_send())
 
 
 def store_kernel(*refs):
@@ -341,7 +352,7 @@
     scratch += [pltpu.VMEM((frames, tokens, width), half)] * 2
     scratch += [pltpu.VMEM((frames, tokens, width), jnp.float32)] * 2
     scratch += [pltpu.SemaphoreType.DMA((3 + 2 * count,))]
-    scratch += [pltpu.SemaphoreType.DMA((count, 4))] * 4
+    scratch += [pltpu.SemaphoreType.DMA((count, 4 + reach))] * 4
     stacked = [pltpu.VMEM((frames, w // head * tokens, w), half) for _, w in tiles]
     probs = [pltpu.VMEM((frames, 2 * tokens, w // head * tokens), half) for _, w in tiles]
     scratch += stacked * 2 + probs * 2

time: 21.5 us -> 19.1 us (0.89)
  the two profiles are of different devices: /device:TPU:0 before, /device:TPU:19 now
where the time goes in v6:
time: 19.1 us; the launch traced here: 18.9 us
  Pallas kernels  18.3 us (96%)
  between operations  0.64 us (3%)
    pallas_call x1, Pallas kernels, body(): pl.pallas_call(functools.partial(kernel, n, reach, tiles, groups, head),...  17.4 us
    pallas_call x1, Pallas kernels, body(): pl.pallas_call(store_kernel, out_shape=like, in_specs=[vmem] * 4, out_spe...  0.87 us

profile of v6, /device:TPU:19, one launch (start us, length us, event | category | flops | bytes accessed | tf_op | source)
XLA Modules:
  0.0 18.9 jit_solution(15121086785827315790)
XLA Ops:
  0.6 17.4 %shard_map.84 = (bf16[4,32,640]{2,1,0:T(8,128)(2,1)S(1)}, bf16[4,32,640]{2,1,0:T(8,128)(2,1)S(1)}, bf16[4,32,640]{2,1,0:T(8,128)(2,1)S(1)}, bf16[4,32,640]{2,1,0:T(8,128)(2,1)S(1)}) custom-call(s32[16]{0:T(128)} %len_ref.1, bf16[4,32,640]{2,1,0:T(8,128)(2,1)} %q_ref.1, bf16[4,32,640]{2,1,0:T(8,128)(2,1)} %k_ref.1, bf16[4,32,640]{2,1,0:T(8,128)(2,1)} %v_ref.1, ...), custom_call_target="tpu_custom_call" | custom-call | tf_op jit(solution)/shard_map/pallas_call | solution.py:378
  18.1 0.9 %shard_map.85 = (bf16[4,32,640]{2,1,0:T(8,128)(2,1)}, bf16[4,32,640]{2,1,0:T(8,128)(2,1)}, bf16[4,32,640]{2,1,0:T(8,128)(2,1)}, bf16[4,32,640]{2,1,0:T(8,128)(2,1)}) custom-call(bf16[4,32,640]{2,1,0:T(8,128)(2,1)S(1)} %get-tuple-element.8.refs_0_, bf16[4,32,640]{2,1,0:T(8,128)(2,1)S(1)} %get-tuple-element.9.refs_1_, ...), custom_call_target="tpu_custom_call" | custom-call | tf_op jit(solution)/shard_map/pallas_call | solution.py:388
